TPU v7x, 256 devices: a whole 4x4x8 slice. The times are simulated.
256 devices in a mesh: pen: 128 (over y_hi, z, x, core), coil: 2 (over y_lo).
Axes of the slice: x: 4, y: 4 (y_hi: 2, y_lo: 2; y = y_hi * 2 + y_lo), z: 8, core: 2. Of those that a mesh axis runs over, the one named last changes fastest.
Arguments:
- image_field: float32 [512, 512, 2, 128], P('pen'), may hold values from -6 to 6
- coil_maps: bfloat16 [2, 512, 512, 2, 128], P('coil', 'pen'), may hold values from -5 to 5
- samples: bfloat16 [2, 4096, 128, 2, 128], P('coil', 'pen'), may hold values from -6 to 6
- kernels: bfloat16 [4096, 128, 128], P('pen'), may hold values from -0.5 to 0.5
- tile_of_block: int32 [4096], P('pen'), may hold values from 0 to 2047, as said below
Outputs:
- gradient: float32 [512, 512, 2, 128], P('pen', 'coil')
Inputs may be any that keep to these rules, and one draw needn't show every extreme that they name: The tile of every block lies with the block: tile_of_block[b] // 16 == b // 32; every tile is named by at least one block.
All inputs are finite; a program needn't handle non-finite values.
Results may differ from a plain program's by a relative error of at most 0.012.
Values may be sent and summed in bfloat16 or wider, within the bound.
A program may use at most 128 MiB of HBM per device.

v0:
```python
import math

import jax
import jax.numpy as jnp
from jax import lax
from jax.sharding import PartitionSpec as P

NL = 512
NZ = 128
TILE = 128


tv_weight = 2.0


def shifted(shard, axis, by):
    length = lax.axis_size(axis)
    pairs = [(i, i + by) for i in range(length) if 0 <= i + by < length]
    return lax.ppermute(shard, axis, pairs)


def dft_tables(length, direction):
    index = lax.iota(jnp.int32, length)
    phase = index[:, None] * index[None, :] % length
    angle = 2.0 * math.pi / length * phase.astype(jnp.float32)
    cosine = jnp.cos(angle) / math.sqrt(length)
    sine = direction * jnp.sin(angle) / math.sqrt(length)
    table = jnp.stack([jnp.stack([cosine, sine], -1), jnp.stack([-sine, cosine], -1)], 1)
    high_part = table.astype(jnp.bfloat16)
    low_part = (table - high_part.astype(jnp.float32)).astype(jnp.bfloat16)
    return (high_part, low_part)


def along_second(tables, values):
    first = jnp.einsum("kpxr,yxrz->ykpz", tables[0], values, preferred_element_type=jnp.float32)
    return first + jnp.einsum(
        "kpxr,yxrz->ykpz", tables[1], values, preferred_element_type=jnp.float32
    )


def along_first(tables, values):
    first = jnp.einsum("kpyr,yxrz->kxpz", tables[0], values, preferred_element_type=jnp.float32)
    return first + jnp.einsum(
        "kpyr,yxrz->kxpz", tables[1], values, preferred_element_type=jnp.float32
    )


def flux_fields(extended, first_row, first_col):
    center = extended[:-1, :-1]
    row_ids = first_row + jnp.arange(center.shape[0])
    col_ids = first_col + jnp.arange(center.shape[1])
    diff_y = (extended[1:, :-1] - center) * (row_ids != NL - 1)[:, None, None, None]
    diff_x = (extended[:-1, 1:] - center) * (col_ids != NL - 1)[None, :, None, None]
    diff_z = jnp.concatenate(
        [center[..., 1:] - center[..., :-1], jnp.zeros_like(center[..., :1])], 3
    )
    norm_den = jnp.sqrt(
        1.0 + jnp.sum(diff_y * diff_y + diff_x * diff_x + diff_z * diff_z, axis=2, keepdims=True)
    )
    inside = ((row_ids >= 0)[:, None] & (col_ids >= 0)[None, :]).astype(jnp.float32)[
        :, :, None, None
    ]
    return (diff_y / norm_den * inside, diff_x / norm_den * inside, diff_z / norm_den * inside)


def plane_divergence(flux_z):
    return jnp.concatenate([jnp.zeros_like(flux_z[..., :1]), flux_z[..., :-1]], 3) - flux_z


def on_device(image_field, coil_maps, samples, kernels, tile_of_block):
    own_rows = image_field.shape[0]
    pen_count = lax.axis_size("pen")
    half_cols = NL // lax.axis_size("coil")
    local_cols = NL // pen_count
    pen_id = lax.axis_index("pen")
    coil_id = lax.axis_index("coil")
    row_start = pen_id * own_rows
    col_start = coil_id * half_cols
    map_real = coil_maps[0, :, :, 0].astype(jnp.float32)
    map_imag = coil_maps[0, :, :, 1].astype(jnp.float32)
    field_real = image_field[:, :, 0]
    field_imag = image_field[:, :, 1]
    coil_image = jnp.stack(
        [
            map_real * field_real - map_imag * field_imag,
            map_real * field_imag + map_imag * field_real,
        ],
        2,
    ).astype(jnp.bfloat16)
    forward_tab = dft_tables(NL, 1.0)
    adjoint_tab = dft_tables(NL, -1.0)
    rows_spectrum = along_second(forward_tab, coil_image).astype(jnp.bfloat16)
    kspace_grid = along_first(
        forward_tab, lax.all_to_all(rows_spectrum, "pen", split_axis=1, concat_axis=0, tiled=True)
    ).astype(jnp.bfloat16)
    grid_tiles = (
        kspace_grid.reshape(NL // TILE, TILE, local_cols, 2 * NZ)
        .transpose(2, 0, 1, 3)
        .reshape(-1, TILE, 2 * NZ)
    )
    tile_count = grid_tiles.shape[0]
    local_ids = tile_of_block - pen_id * tile_count
    picked = jnp.take(grid_tiles, local_ids, axis=0)
    predicted = jnp.einsum("bst,btc->bsc", kernels, picked, preferred_element_type=jnp.float32)
    measured = samples[0].reshape(predicted.shape).astype(jnp.float32)
    misfit = (predicted - measured).astype(jnp.bfloat16)
    back_terms = jnp.einsum("bst,bsc->btc", kernels, misfit, preferred_element_type=jnp.float32)
    onehot = (local_ids[:, None] == jnp.arange(tile_count, dtype=jnp.int32)[None, :]).astype(
        jnp.float32
    )
    back_tiles = jnp.einsum(
        "bl,btc->ltc", onehot, back_terms, precision=lax.Precision.HIGHEST
    ).astype(jnp.bfloat16)
    back_grid = (
        back_tiles.reshape(local_cols, NL // TILE, TILE, 2 * NZ)
        .transpose(1, 2, 0, 3)
        .reshape(NL, local_cols, 2, NZ)
    )
    back_rows = along_first(adjoint_tab, back_grid).astype(jnp.bfloat16)
    back_image = along_second(
        adjoint_tab, lax.all_to_all(back_rows, "pen", split_axis=0, concat_axis=1, tiled=True)
    )
    back_real = back_image[:, :, 0]
    back_imag = back_image[:, :, 1]
    coil_term = jnp.stack(
        [map_real * back_real + map_imag * back_imag, map_real * back_imag - map_imag * back_real],
        2,
    )
    summed = lax.psum(coil_term, "coil")
    data_gradient = lax.dynamic_slice_in_dim(summed, col_start, half_cols, 1)
    padded = jnp.pad(image_field, ((0, 0), (1, 1), (0, 0), (0, 0)))
    window = lax.dynamic_slice_in_dim(padded, col_start, half_cols + 2, 1)
    upper_row = shifted(window[:1], "pen", -1)
    extended = jnp.concatenate([window, upper_row], 0)
    flux_y, flux_x, flux_z = flux_fields(extended, row_start, col_start - 1)
    lower_row = shifted(flux_y[-1:], "pen", 1)
    flux_before = jnp.concatenate([lower_row, flux_y[:-1]], 0)
    tv_part = (
        flux_before[:, 1:]
        - flux_y[:, 1:]
        + flux_x[:, :-1]
        - flux_x[:, 1:]
        + plane_divergence(flux_z[:, 1:])
    )
    return data_gradient + tv_weight * tv_part


def solution(mesh):
    in_specs = (
        P("pen", None, None, None),
        P("coil", "pen", None, None, None),
        P("coil", "pen", None, None, None),
        P("pen", None, None),
        P("pen"),
    )
    out_specs = P("pen", "coil", None, None)
    return jax.shard_map(
        on_device, mesh=mesh, in_specs=in_specs, out_specs=out_specs, check_vma=False
    )
```

profile of v0, /device:TPU:1, one launch (start us, length us, event | category | flops | bytes accessed | tf_op | source)
XLA Modules:
  0.0 271.2 jit_solution(11424692795102408976)
XLA Ops:
  6.5 5.1 %cosine_multiply_fusion = (f32[512,512,1]{1,0,2:T(8,128)}, f32[512,512,1]{1,0,2:T(8,128)}) fusion(), kind=kLoop, calls=%fused_computation.86 | loop fusion | flops 4194304 | bytes 2097152 | tf_op jit(solution)/shard_map/div | solution.py:26
  11.6 4.8 %broadcast_multiply_fusion.1 = (f32[512,512,1]{1,0,2:T(8,128)}, f32[512,512,1]{1,0,2:T(8,128)}) fusion(), kind=kLoop, calls=%fused_computation.93 | loop fusion | flops 4194304 | bytes 2097152 | tf_op jit(solution)/shard_map/div | solution.py:27
  16.4 4.6 %fusion.50 = f32[512,512,1]{1,0,2:T(8,128)} fusion(), kind=kLoop, calls=%fused_computation.96 | loop fusion | flops 4194304 | bytes 1048576 | tf_op jit(solution)/shard_map/neg | solution.py:28
  21.0 2.7 %copy.32 = f32[4,512,2,128]{1,3,2,0:T(8,128)S(1)} copy(f32[4,512,2,128]{3,2,1,0:T(2,128)} %param.5) | data formatting | bytes 4194304 | tf_op args[0]
  23.8 4.3 %fusion.80 = (bf16[1,4,512,1,128]{4,3,2,1,0:T(2,128)(2,1)}, bf16[1,4,512,1,128]{4,3,2,1,0:T(2,128)(2,1)}) fusion(bf16[1,4,512,2,128]{4,3,2,1,0:T(2,128)(2,1)} %param.6), kind=kLoop, calls=%fused_computation.125 | loop fusion | bytes 2097152 | tf_op jit(solution)/shard_map/slice | solution.py:79
  28.0 3.5 %copy.75 = bf16[1,4,512,1,128]{2,4,1,3,0:T(8,128)(2,1)} copy(bf16[1,4,512,1,128]{4,3,2,1,0:T(2,128)(2,1)} %get-tuple-element.17) | data formatting | bytes 1048576
  31.5 3.5 %copy.76 = bf16[1,4,512,1,128]{2,4,1,3,0:T(8,128)(2,1)} copy(bf16[1,4,512,1,128]{4,3,2,1,0:T(2,128)(2,1)} %get-tuple-element.18) | data formatting | bytes 1048576
  35.0 1.7 fusion.31
  36.8 0.1 copy-done.17
  36.9 0.3 copy-done.18
  37.2 0.3 copy-done.19
  37.5 4.5 %fusion.8 = (f32[512,1,512,2]{2,0,3,1:T(8,128)}, f32[512,1,512,2]{2,0,3,1:T(8,128)}, f32[512,1,512,2]{2,0,3,1:T(8,128)S(1)}, f32[512,1,512,2]{2,0,3,1:T(8,128)S(1)}) fusion(f32[512,512,1]{1,0,2:T(8,128)S(1)} %copy-done.16, f32[512,512,1]{1,0,2:T(8,128)S(1)} %copy-done.17, f32[512,512,1]{1,0,2:T(8,128)} %fusion.50, f32[512,512,1]{1,0,2:T(8,128)S(1)} %copy-done.19, ...), kind=kLoop, calls=%fused_computation.25 | loop fusion | flops 2097152 | bytes 13631488 | tf_op jit(solution)/shard_map/stack | solution.py:28
  42.0 1.3 fusion.47
  43.3 0.1 copy-done.10
  43.4 0.6 copy-done.12
  44.0 2.3 fusion.24
  46.3 3.7 %copy.35 = bf16[4,512,2,128]{3,2,0,1:T(2,128)(2,1)} copy(bf16[4,512,2,128]{1,3,2,0:T(8,128)(2,1)} %fusion.24) | data formatting | bytes 2097152 | tf_op jit(solution)/shard_map/convert_element_type | solution.py:92
  49.9 16.9 %all-to-all-start = ((bf16[4,512,2,128]{3,2,0,1:T(2,128)(2,1)}), bf16[4,512,2,128]{3,2,0,1:T(2,128)(2,1)}, u32[]{:S(2)}, u32[]{:S(2)}) async-start(bf16[4,512,2,128]{3,2,0,1:T(2,128)(2,1)} %copy.35), calls=%async_computation | async-start | bytes 2097152 | tf_op jit(solution)/shard_map/all_to_all | solution.py:94
  66.8 6.7 %copy.42 = f32[1,32,128,2,128]{2,4,3,1,0:T(8,128)} copy(bf16[1,32,128,2,128]{4,3,2,1,0:T(2,128)(2,1)} %param.7) | data formatting | bytes 6291456 | tf_op jit(solution)/shard_map/convert_element_type | solution.py:105
  73.6 26.0 %all-to-all-done = bf16[4,512,2,128]{3,2,0,1:T(2,128)(2,1)} async-done(((bf16[4,512,2,128]{3,2,0,1:T(2,128)(2,1)}), bf16[4,512,2,128]{3,2,0,1:T(2,128)(2,1)}, u32[]{:S(2)}, u32[]{:S(2)}) %all-to-all-start) | async-done | bytes 1048608 | tf_op jit(solution)/shard_map/all_to_all | solution.py:94
  99.6 1.5 copy.36
  101.1 0.8 copy.37
  101.9 0.2 copy-done.13
  102.1 1.3 fusion.58
  103.4 2.3 fusion.25
  105.7 2.2 reshape.212
  107.9 2.3 copy.40
  110.2 3.2 %gather_fusion = bf16[32,128,256]{2,1,0:T(8,128)(2,1)} fusion(bf16[16,128,256]{2,1,0:T(8,128)(2,1)} %bitcast.149, s32[1024]{0:T(1024)S(1)} %pad_clamp_fusion), kind=kCustom, calls=%fused_computation | custom fusion | bytes 4194432 | tf_op jit(solution)/shard_map/jit(_take)/gather | solution.py:103
  113.4 6.4 %convolution_bitcast_fusion = f32[32,128,256]{1,2,0:T(8,128)} fusion(bf16[32,128,128]{2,1,0:T(8,128)(2,1)S(1)} %copy-done, f32[32,128,256]{1,2,0:T(8,128)} %bitcast.148, bf16[32,128,256]{2,1,0:T(8,128)(2,1)} %gather_fusion, pred[32]{0:T(512)(128)(4,1)S(1)} %get-tuple-element.5), kind=kOutput, calls=%fused_computation.21 | convolution fusion | flops 540016640 | bytes 11534368 | tf_op jit(solution)/shard_map/bst,bsc->btc/dot_general | solution.py:107
  119.8 5.5 %copy.43 = f32[32,128,256]{2,0,1:T(8,128)} copy(f32[32,128,256]{1,2,0:T(8,128)} %convolution_bitcast_fusion) | data formatting | bytes 8388608 | tf_op jit(solution)/shard_map/bst,bsc->btc/dot_general | solution.py:107
  125.3 4.7 %convolution_convert_fusion = bf16[16,128,256]{2,0,1:T(8,128)(2,1)} fusion(f32[32,128,256]{2,0,1:T(8,128)} %copy.43, s32[32]{0:T(128)S(1)} %get-tuple-element.6), kind=kOutput, calls=%fused_computation.60 | convolution fusion | flops 201851392 | bytes 5243008 | tf_op jit(solution)/shard_map/bl,btc->ltc/dot_general | solution.py:111
  130.0 1.3 reshape.214
  131.4 2.2 copy.44
  133.5 1.5 reshape.238
  135.0 3.7 %fusion.40 = f32[4,128,512,2,1]{2,1,4,3,0:T(8,128)S(1)} fusion(bf16[512,4,2,128,1]{0,3,2,1,4:T(8,128)(2,1)S(1)} %reshape.238, f32[512,1,512,2]{2,0,3,1:T(8,128)} %get-tuple-element.14, f32[512,1,512,2]{2,0,3,1:T(8,128)} %get-tuple-element.13), kind=kOutput, calls=%fused_computation.83 | convolution fusion | flops 1077936128 | bytes 7340032 | tf_op jit(solution)/shard_map/kpyr,yxrz->kxpz/dot_general | solution.py:42
  138.7 2.3 fusion.26
  141.0 3.7 %copy.45 = bf16[512,4,2,128]{3,2,1,0:T(2,128)(2,1)} copy(bf16[512,4,2,128]{0,3,2,1:T(8,128)(2,1)} %fusion.26) | data formatting | bytes 2097152 | tf_op jit(solution)/shard_map/convert_element_type | solution.py:119
  144.7 5.5 %all-to-all-start.1 = ((bf16[512,4,2,128]{3,2,1,0:T(2,128)(2,1)}), bf16[512,4,2,128]{3,2,1,0:T(2,128)(2,1)S(1)}, u32[]{:S(2)}, u32[]{:S(2)}) async-start(bf16[512,4,2,128]{3,2,1,0:T(2,128)(2,1)} %copy.45), calls=%async_computation.1 | async-start | bytes 2097152 | tf_op jit(solution)/shard_map/all_to_all | solution.py:121
  150.2 0.0 all-reduce.5.cloned.1.call-start
  150.3 0.9 pad_dynamic-slice_fusion.4
  151.2 2.2 collective-permute-start
  153.4 29.4 %all-to-all-done.1 = bf16[512,4,2,128]{3,2,1,0:T(2,128)(2,1)S(1)} async-done(((bf16[512,4,2,128]{3,2,1,0:T(2,128)(2,1)}), bf16[512,4,2,128]{3,2,1,0:T(2,128)(2,1)S(1)}, u32[]{:S(2)}, u32[]{:S(2)}) %all-to-all-start.1) | async-done | bytes 1048608 | tf_op jit(solution)/shard_map/all_to_all | solution.py:121
  182.8 0.1 copy.46
  182.9 0.8 copy.47
  183.7 0.6 copy-done.3
  184.4 0.6 copy-done.5
  185.0 1.3 fusion.55
  186.3 1.3 fusion.11
  187.6 0.4 fusion.34
  188.1 1.5 pad_maximum_fusion.6
  189.6 1.6 pad_dynamic-slice_fusion.5
  191.2 2.0 fusion.21
  193.3 0.1 and_convert_fusion
  193.4 3.1 %add_reduce_fusion = f32[4,257,128]{1,2,0:T(8,128)S(1)} fusion(f32[4,257,2,127]{1,3,2,0:T(8,128)} %fusion.21, f32[257]{0:T(512)S(1)} %get-tuple-element.21, s32[]{:T(128)S(6)} %select_n.65, f32[4,512,2,128]{1,3,2,0:T(8,128)S(1)} %copy.32, s32[]{:T(128)S(6)} %add.171, f32[4]{0:T(128)S(1)} %get-tuple-element.22, ...), kind=kLoop, calls=%fused_computation.56 | loop fusion | flops 2763264 | bytes 4989948 | tf_op jit(solution)/shard_map/reduce_sum | solution.py:58
  196.5 0.2 add_sqrt_fusion
  196.7 1.2 copy-done.6
  197.9 3.1 %divide_multiply_fusion.2 = (f32[4,257,2,128]{1,3,2,0:T(8,128)S(1)}, f32[4,257,2,128]{1,3,2,0:T(8,128)}, f32[4,257,2,128]{1,3,2,0:T(8,128)}) fusion(f32[4,257]{1,0:T(4,128)S(1)} %and_convert_fusion, f32[4,257,128]{1,2,0:T(8,128)S(1)} %add_sqrt_fusion, f32[4]{0:T(128)S(1)} %get-tuple-element.22, s32[]{:T(128)S(6)} %select_n.65, ...), kind=kLoop, calls=%fused_computation.55 | loop fusion | flops 2894848 | bytes 8152076 | tf_op jit(solution)/shard_map/mul | solution.py:63
  201.0 1.2 copy-done.8
  202.3 1.9 collective-permute-start.1
  204.2 2.5 slice.90
  206.7 2.8 %slice.94 = f32[4,256,2,127]{1,3,2,0:T(8,128)} slice(f32[4,257,2,128]{1,3,2,0:T(8,128)} %get-tuple-element.19), slice={[0:4], [1:257], [0:2], [0:127]} | slice | bytes 2080768 | tf_op jit(solution)/shard_map/slice | solution.py:67
  209.5 47.2 %all-reduce.5.cloned.1.call-done = f32[4,512,2,128]{1,3,2,0:T(8,128)} async-done(((f32[4,512,2,128]{1,3,2,0:T(8,128)}), f32[4,512,2,128]{1,3,2,0:T(8,128)}) %all-reduce.5.cloned.1.call-update) | async-done | bytes 2097168 | tf_op jit(solution)/shard_map/psum | solution.py:129
  256.7 5.5 %fusion.38 = f32[4,256,2,128]{1,3,2,0:T(8,128)} fusion(f32[4,257,2,128]{1,3,2,0:T(8,128)} %get-tuple-element.19, f32[4,257,2,128]{1,3,2,0:T(8,128)} %get-tuple-element.12, f32[4,257,2,128]{1,3,2,0:T(8,128)S(1)} %copy-done.9, f32[3,257,2,128]{1,3,2,0:T(8,128)} %slice.90, f32[1,257,2,128]{1,3,2,0:T(8,128)S(1)} %collective-permute-done.1, ...), kind=kLoop, calls=%fused_computation.76 | loop fusion | flops 2097152 | bytes 8384516 | tf_op jit(solution)/shard_map/add | solution.py:145
  262.1 2.2 copy.51
  (41 shorter events, 0.1 us)
Async XLA Ops:
  6.5 106.9 %copy-start = (bf16[32,128,128]{2,1,0:T(8,128)(2,1)S(1)}, bf16[32,128,128]{2,1,0:T(8,128)(2,1)}, u32[]{:S(2)}) copy-start(bf16[32,128,128]{2,1,0:T(8,128)(2,1)} %param.8) | copy-start | bytes 3145732
  35.0 1.8 copy-start.16
  35.0 1.9 copy-start.17
  35.0 2.2 copy-start.18
  35.0 2.5 copy-start.19
  42.0 1.4 copy-start.10
  42.0 2.0 copy-start.12
  49.9 49.7 %all-to-all-start = ((bf16[4,512,2,128]{3,2,0,1:T(2,128)(2,1)}), bf16[4,512,2,128]{3,2,0,1:T(2,128)(2,1)}, u32[]{:S(2)}, u32[]{:S(2)}) async-start(bf16[4,512,2,128]{3,2,0,1:T(2,128)(2,1)} %copy.35), calls=%async_computation | async-start | bytes 2097152 | tf_op jit(solution)/shard_map/all_to_all | solution.py:94
  66.8 6.7 %copy-start.20 = (s32[32]{0:T(128)S(1)}, s32[32]{0:T(128)}, u32[]{:S(2)}) copy-start(s32[32]{0:T(128)} %param.9) | copy-start | bytes 388
  99.6 2.3 copy-start.11
  99.6 2.5 copy-start.13
  135.0 3.7 %copy-start.2 = (f32[512,1,512,2]{2,0,3,1:T(8,128)S(1)}, f32[512,1,512,2]{2,0,3,1:T(8,128)}, u32[]{:S(2)}) copy-start(f32[512,1,512,2]{2,0,3,1:T(8,128)} %get-tuple-element.13) | copy-start | bytes 6291460
  135.0 3.7 %copy-start.4 = (f32[512,1,512,2]{2,0,3,1:T(8,128)S(1)}, f32[512,1,512,2]{2,0,3,1:T(8,128)}, u32[]{:S(2)}) copy-start(f32[512,1,512,2]{2,0,3,1:T(8,128)} %get-tuple-element.14) | copy-start | bytes 6291460
  144.7 38.1 %all-to-all-start.1 = ((bf16[512,4,2,128]{3,2,1,0:T(2,128)(2,1)}), bf16[512,4,2,128]{3,2,1,0:T(2,128)(2,1)S(1)}, u32[]{:S(2)}, u32[]{:S(2)}) async-start(bf16[512,4,2,128]{3,2,1,0:T(2,128)(2,1)} %copy.45), calls=%async_computation.1 | async-start | bytes 2097152 | tf_op jit(solution)/shard_map/all_to_all | solution.py:121
  150.2 106.4 %all-reduce.5.cloned.1.call-start = ((), (), s32[]{:S(2)}) async-start(), calls=%async_computation.2 | async-start | bytes 4194304 | tf_op jit(solution)/shard_map/psum | solution.py:129
  151.2 42.1 %collective-permute-start = (f32[1,258,2,128]{1,3,2,0:T(8,128)}, f32[1,258,2,128]{1,3,2,0:T(8,128)S(1)}, u32[]{:S(2)}, u32[]{:S(2)}) collective-permute-start(f32[1,258,2,128]{1,3,2,0:T(8,128)} %pad_dynamic-slice_fusion.4), channel_id=1, source_target_pairs={{2,0},{4,2},{6,4},{8,6},{10,8},{12,10},{14,12},{16,14},{18,16},{20... | collective-permute-start | bytes 792584 | tf_op jit(solution)/shard_map/ppermute | solution.py:19
  182.8 1.6 copy-start.3
  182.8 2.2 copy-start.5
  186.3 1.3 copy-start.14
  186.3 1.3 copy-start.15
  193.4 3.4 %copy-start.7 = (f32[4,257,2,127]{1,3,2,0:T(8,128)S(1)}, f32[4,257,2,127]{1,3,2,0:T(8,128)}, u32[]{:S(2)}) copy-start(f32[4,257,2,127]{1,3,2,0:T(8,128)} %fusion.21) | copy-start | bytes 3133348
  196.5 1.4 copy-start.6
  201.0 1.2 copy-start.8
  202.3 7.2 %collective-permute-start.1 = (f32[1,257,2,128]{1,3,2,0:T(8,128)S(1)}, f32[1,257,2,128]{1,3,2,0:T(8,128)S(1)}, u32[]{:S(2)}, u32[]{:S(2)}) collective-permute-start(f32[1,257,2,128]{1,3,2,0:T(8,128)S(1)} %slice.89), channel_id=1, source_target_pairs={{0,2},{2,4},{4,6},{6,8},{8,10},{10,12},{12,14},{14,16},{16,18},{18... | collective-permute-start | bytes 789512 | tf_op jit(solution)/shard_map/ppermute | solution.py:19
  204.2 52.4 %copy-start.9 = (f32[4,257,2,128]{1,3,2,0:T(8,128)S(1)}, f32[4,257,2,128]{1,3,2,0:T(8,128)}, u32[]{:S(2)}) copy-start(f32[4,257,2,128]{1,3,2,0:T(8,128)} %copy-done.8) | copy-start | bytes 3158020
  256.7 7.7 %copy-start.1 = (bf16[32,128,128]{2,1,0:T(8,128)(2,1)S(1)}, bf16[32,128,128]{2,1,0:T(8,128)(2,1)}, u32[]{:S(2)}) copy-start(bf16[32,128,128]{2,1,0:T(8,128)(2,1)} %param.8) | copy-start | bytes 3145732
Sparse Core Ops, SparseCore 0:
  189.7 66.8 all-reduce.4
where the time goes:
time: 272 us; the launch traced here: 271 us
  waiting for transfers between devices  103 us (38%)
  local copies, waits for them, and re-layouts  64.8 us (24%)
  other arithmetic  36.7 us (13%)
  matrix products  26.8 us (10%)
  starting transfers between devices  26.6 us (10%)
  between operations  13.7 us (5%)
    psum x1, waiting for transfers between devices, on_device(): summed = lax.psum(coil_term, 'coil')  47.2 us
    all_to_all x1, waiting for transfers between devices, on_device(): lax.all_to_all(back_rows, 'pen', split_axis=0, concat_axis=1, tiled=True)  29.4 us
    all_to_all x1, waiting for transfers between devices, on_device(): lax.all_to_all(rows_spectrum, 'pen', split_axis=1, concat_axis=0, tiled=T...  26 us
    all_to_all x1, starting transfers between devices, on_device(): lax.all_to_all(rows_spectrum, 'pen', split_axis=1, concat_axis=0, tiled=T...  16.9 us
    unnamed x45, local copies, waits for them, and re-layouts  15.1 us
    convert_element_type x1, local copies, waits for them, and re-layouts, on_device(): measured = samples[0].reshape(predicted.shape).astype(jnp.float32)  6.67 us
    dot_general x1, matrix products, on_device(): jnp.einsum('bst,bsc->btc', kernels, misfit, preferred_element_type=jnp.fl...  6.36 us
    all_to_all x1, starting transfers between devices, on_device(): lax.all_to_all(back_rows, 'pen', split_axis=0, concat_axis=1, tiled=True)  5.54 us
  transfers between devices with their start and end apart: 5, of which 3 were waited for; matrix products, arithmetic and copies ran while one was open for 11% of the time, Pallas kernels for 0%

commit v1 on v0

--- a/solution.py
+++ b/solution.py
@@ -3,6 +3,8 @@
 import jax
 import jax.numpy as jnp
 from jax import lax
+from jax.experimental import pallas as pl
+from jax.experimental.pallas import tpu as pltpu
 from jax.sharding import PartitionSpec as P
 
 NL = 512
@@ -17,6 +19,59 @@
     length = lax.axis_size(axis)
     pairs = [(i, i + by) for i in range(length) if 0 <= i + by < length]
     return lax.ppermute(shard, axis, pairs)
+
+
+def exchange_kernel(blocks_ref, out_ref, send_sem, recv_sem, own_sem):
+    me = lax.axis_index("pen")
+    coil = lax.axis_index("coil")
+    y, z, rest = me // 64, me // 8 % 8, me % 8
+
+    def partner(i):
+        step = i + 1
+        dz, other = step % 8, step // 8
+        return (y + other // 8) % 2 * 64 + (z + dz) % 8 * 8 + (rest + other % 8) % 8
+
+    barrier = pltpu.get_barrier_semaphore()
+
+    def greet(i, carry):
+        pl.semaphore_signal(
+            barrier, inc=1, device_id=(partner(i), coil), device_id_type=pl.DeviceIdType.MESH
+        )
+        return carry
+
+    lax.fori_loop(0, 127, greet, 0)
+    own = pltpu.make_async_copy(blocks_ref.at[me], out_ref.at[me], own_sem)
+    own.start()
+    pl.semaphore_wait(barrier, 127)
+
+    def send(i, carry):
+        d = partner(i)
+        pltpu.make_async_remote_copy(
+            blocks_ref.at[d],
+            out_ref.at[me],
+            send_sem,
+            recv_sem,
+            device_id=(d, coil),
+            device_id_type=pl.DeviceIdType.MESH,
+        ).start()
+        return carry
+
+    lax.fori_loop(0, 127, send, 0)
+    own.wait()
+    part = out_ref.at[pl.ds(0, 127)]
+    pltpu.make_async_copy(part, part, recv_sem).wait()
+    pltpu.make_async_copy(part, part, send_sem).wait()
+
+
+def exchange(blocks):
+    return pl.pallas_call(
+        exchange_kernel,
+        out_shape=jax.ShapeDtypeStruct(blocks.shape, blocks.dtype),
+        in_specs=[pl.BlockSpec(memory_space=pltpu.VMEM)],
+        out_specs=pl.BlockSpec(memory_space=pltpu.VMEM),
+        scratch_shapes=[pltpu.SemaphoreType.DMA] * 3,
+        compiler_params=pltpu.CompilerParams(collective_id=0, has_side_effects=True),
+    )(blocks)
 
 
 def dft_tables(length, direction):
@@ -91,7 +146,9 @@
     adjoint_tab = dft_tables(NL, -1.0)
     rows_spectrum = along_second(forward_tab, coil_image).astype(jnp.bfloat16)
     kspace_grid = along_first(
-        forward_tab, lax.all_to_all(rows_spectrum, "pen", split_axis=1, concat_axis=0, tiled=True)
+        forward_tab, exchange(
+            rows_spectrum.reshape(4, 128, 4, 256).transpose(1, 0, 2, 3).reshape(128, 16, 256)
+        ).reshape(512, 4, 2, 128)
     ).astype(jnp.bfloat16)
     grid_tiles = (
         kspace_grid.reshape(NL // TILE, TILE, local_cols, 2 * NZ)
@@ -118,7 +175,10 @@
     )
     back_rows = along_first(adjoint_tab, back_grid).astype(jnp.bfloat16)
     back_image = along_second(
-        adjoint_tab, lax.all_to_all(back_rows, "pen", split_axis=0, concat_axis=1, tiled=True)
+        adjoint_tab, exchange(back_rows.reshape(128, 16, 256))
+        .reshape(128, 4, 4, 256)
+        .transpose(1, 0, 2, 3)
+        .reshape(4, 512, 2, 128)
     )
     back_real = back_image[:, :, 0]
     back_imag = back_image[:, :, 1]

time: 272 us -> 301 us (1.11)
  Pallas kernels: 0 us -> 81.2 us
  waiting for transfers between devices: 103 us -> 50.5 us
  starting transfers between devices: 26.6 us -> 4.48 us
  local copies, waits for them, and re-layouts: 64.8 us -> 79.3 us
  matrix products: 26.8 us -> 33 us
    pallas_call x0 -> x2, Pallas kernels: none -> 81.2 us  [exchange(): pl.pallas_call(exchange_kernel, out_shape=jax.ShapeDtypeStruct(blocks.sha...]
    all_to_all x2 -> x0, waiting for transfers between devices: 55.4 us -> none  [the longest x1 29.4 us: on_device(): lax.all_to_all(back_rows, 'pen', split_axis=0, concat_axis=1, tiled=True)]
    all_to_all x2 -> x0, starting transfers between devices: 22.4 us -> none  [the longest x1 16.9 us: on_device(): lax.all_to_all(rows_spectrum, 'pen', split_axis=1, concat_axis=0, tiled=T...]
    reshape x0 -> x9, local copies, waits for them, and re-layouts: none -> 19.3 us  [the longest x4 7.38 us: on_device(): back_image = along_second(adjoint_tab, exchange(back_rows.reshape(128, 16...]
    all_to_all x4 -> x0, local copies, waits for them, and re-layouts: 3.27 us -> none  [the longest x2 2.32 us: on_device(): lax.all_to_all(rows_spectrum, 'pen', split_axis=1, concat_axis=0, tiled=T...]
    unnamed x45 -> x49, local copies, waits for them, and re-layouts: 15.1 us -> 14.6 us
  transfers between devices with their start and end apart: 5 -> 3, of which waited for: 3 -> 2; matrix products, arithmetic and copies ran while one was open for 11% -> 5% of each run, Pallas kernels for 0% -> 0%
where the time goes in v1:
time: 301 us; the launch traced here: 299 us
  Pallas kernels  81.2 us (27%)
  local copies, waits for them, and re-layouts  79.3 us (26%)
  waiting for transfers between devices  50.5 us (17%)
  other arithmetic  37.2 us (12%)
  matrix products  33 us (11%)
  between operations  13.7 us (5%)
  starting transfers between devices  4.48 us (1%)
    pallas_call x2, Pallas kernels, exchange(): pl.pallas_call(exchange_kernel, out_shape=jax.ShapeDtypeStruct(blocks.sha...  81.2 us
    psum x1, waiting for transfers between devices, on_device(): summed = lax.psum(coil_term, 'coil')  47.7 us
    unnamed x49, local copies, waits for them, and re-layouts  14.6 us
    dot_general x2, matrix products, along_first(): jnp.einsum('kpyr,yxrz->kxpz', tables[0], values, preferred_element_type=j...  7.63 us
    reshape x4, local copies, waits for them, and re-layouts, on_device(): back_image = along_second(adjoint_tab, exchange(back_rows.reshape(128, 16...  7.38 us
    dot_general x1, matrix products, on_device(): jnp.einsum('bst,bsc->btc', kernels, misfit, preferred_element_type=jnp.fl...  6.22 us
  transfers between devices with their start and end apart: 3, of which 2 were waited for; matrix products, arithmetic and copies ran while one was open for 5% of the time, Pallas kernels for 0%

profile of v1, /device:TPU:1, one launch (start us, length us, event | category | flops | bytes accessed | tf_op | source)
XLA Modules:
  0.0 299.3 jit_solution(18437070877136081339)
XLA Ops:
  6.5 5.1 %cosine_multiply_fusion = (f32[512,512,1]{1,0,2:T(8,128)}, f32[512,512,1]{1,0,2:T(8,128)}) fusion(), kind=kLoop, calls=%fused_computation.89 | loop fusion | flops 4194304 | bytes 2097152 | tf_op jit(solution)/shard_map/div | solution.py:81
  11.6 4.8 %broadcast_multiply_fusion.1 = (f32[512,512,1]{1,0,2:T(8,128)}, f32[512,512,1]{1,0,2:T(8,128)}) fusion(), kind=kLoop, calls=%fused_computation.96 | loop fusion | flops 4194304 | bytes 2097152 | tf_op jit(solution)/shard_map/div | solution.py:82
  16.4 4.7 %fusion.56 = f32[512,512,1]{1,0,2:T(8,128)} fusion(), kind=kLoop, calls=%fused_computation.99 | loop fusion | flops 4194304 | bytes 1048576 | tf_op jit(solution)/shard_map/neg | solution.py:83
  21.0 2.7 copy.19
  23.8 4.3 %fusion.86 = (bf16[1,4,512,1,128]{4,3,2,1,0:T(2,128)(2,1)}, bf16[1,4,512,1,128]{4,3,2,1,0:T(2,128)(2,1)}) fusion(bf16[1,4,512,2,128]{4,3,2,1,0:T(2,128)(2,1)} %param.6), kind=kLoop, calls=%fused_computation.128 | loop fusion | bytes 2097152 | tf_op jit(solution)/shard_map/slice | solution.py:134
  28.1 3.5 %copy.57 = bf16[1,4,512,1,128]{2,4,1,3,0:T(8,128)(2,1)} copy(bf16[1,4,512,1,128]{4,3,2,1,0:T(2,128)(2,1)} %get-tuple-element.17) | data formatting | bytes 1048576
  31.5 3.5 %copy.58 = bf16[1,4,512,1,128]{2,4,1,3,0:T(8,128)(2,1)} copy(bf16[1,4,512,1,128]{4,3,2,1,0:T(2,128)(2,1)} %get-tuple-element.18) | data formatting | bytes 1048576
  35.0 1.7 fusion.37
  36.8 0.1 copy-done.19
  36.9 0.3 copy-done.20
  37.2 0.3 copy-done.21
  37.5 4.5 %fusion.10 = (f32[512,1,512,2]{2,0,3,1:T(8,128)}, f32[512,1,512,2]{2,0,3,1:T(8,128)}, f32[512,1,512,2]{2,0,3,1:T(8,128)S(1)}, f32[512,1,512,2]{2,0,3,1:T(8,128)S(1)}) fusion(f32[512,512,1]{1,0,2:T(8,128)S(1)} %copy-done.18, f32[512,512,1]{1,0,2:T(8,128)S(1)} %copy-done.19, f32[512,512,1]{1,0,2:T(8,128)} %fusion.56, f32[512,512,1]{1,0,2:T(8,128)S(1)} %copy-done.21, ...), kind=kLoop, calls=%fused_computation.26 | loop fusion | flops 2097152 | bytes 13631488 | tf_op jit(solution)/shard_map/stack | solution.py:83
  42.0 1.3 fusion.53
  43.4 0.6 copy-done.12
  44.0 2.3 fusion.30
  46.3 3.7 %copy.22 = bf16[4,512,2,128]{3,2,1,0:T(2,128)(2,1)} copy(bf16[4,512,2,128]{1,3,2,0:T(8,128)(2,1)} %fusion.30) | data formatting | bytes 2097152 | tf_op jit(solution)/shard_map/convert_element_type | solution.py:147
  49.9 2.5 reshape.230
  52.4 2.6 copy.23
  55.0 2.1 reshape.231.blocks_ref
  57.2 43.0 %shard_map.55 = bf16[128,16,256]{2,1,0:T(8,128)(2,1)} custom-call(bf16[128,16,256]{2,1,0:T(8,128)(2,1)} %reshape.231.blocks_ref), custom_call_target="tpu_custom_call" | custom-call | tf_op jit(solution)/shard_map/pallas_call | solution.py:67
  100.2 2.1 reshape.232
  102.3 3.7 %copy.37 = bf16[512,4,2,128,1]{0,3,2,4,1:T(8,128)(2,1)} copy(bf16[512,4,2,128,1]{3,2,1,0,4:T(2,128)(2,1)} %bitcast.141) | data formatting | bytes 2097152 | tf_op jit(solution)/shard_map/reshape | solution.py:151
  106.0 4.0 %fusion.64 = f32[4,128,512,2,1]{2,1,4,3,0:T(8,128)S(1)} fusion(bf16[512,4,2,128,1]{0,3,2,4,1:T(8,128)(2,1)} %copy.37, f32[512,1,512,2]{2,0,3,1:T(8,128)} %copy-done.10, f32[512,1,512,2]{2,0,3,1:T(8,128)} %copy-done.12), kind=kOutput, calls=%fused_computation.101 | convolution fusion | flops 1077936128 | bytes 7340032 | tf_op jit(solution)/shard_map/kpyr,yxrz->kxpz/dot_general | solution.py:97
  110.1 2.3 fusion.31
  112.3 2.2 reshape.233
  114.5 2.3 copy.26
  116.8 4.9 %reshape.242 = f32[32,128,256]{2,1,0:T(8,128)} reshape(bf16[1,32,128,2,128]{4,3,2,1,0:T(2,128)(2,1)} %param.7) | data formatting | bytes 6291456 | tf_op jit(solution)/shard_map/convert_element_type | solution.py:162
  121.8 3.2 %gather_fusion = bf16[32,128,256]{2,1,0:T(8,128)(2,1)} fusion(bf16[16,128,256]{2,1,0:T(8,128)(2,1)} %bitcast.139, s32[1024]{0:T(1024)S(1)} %pad_clamp_fusion), kind=kCustom, calls=%fused_computation | custom fusion | bytes 4194432 | tf_op jit(solution)/shard_map/jit(_take)/gather | solution.py:160
  125.0 6.2 %fusion.20 = f32[32,256,128]{2,1,0:T(8,128)} fusion(bf16[32,128,128]{2,1,0:T(8,128)(2,1)S(1)} %copy-done, f32[32,128,256]{2,1,0:T(8,128)} %reshape.242, bf16[32,128,256]{2,1,0:T(8,128)(2,1)} %gather_fusion, pred[32]{0:T(512)(128)(4,1)S(1)} %get-tuple-element.5), kind=kOutput, calls=%fused_computation.48 | convolution fusion | flops 540016640 | bytes 11534368 | tf_op jit(solution)/shard_map/bst,bsc->btc/dot_general | solution.py:164
  131.2 5.5 %copy.41 = f32[32,256,128]{1,0,2:T(8,128)} copy(f32[32,256,128]{2,1,0:T(8,128)} %fusion.20) | data formatting | bytes 8388608 | tf_op jit(solution)/shard_map/bst,bsc->btc/dot_general | solution.py:164
  136.7 4.7 %fusion.27 = bf16[16,128,256]{2,0,1:T(8,128)(2,1)} fusion(f32[32,256,128]{1,0,2:T(8,128)} %copy.41, s32[32]{0:T(128)S(1)} %get-tuple-element.6), kind=kOutput, calls=%fused_computation.62 | convolution fusion | flops 201851392 | bytes 5243008 | tf_op jit(solution)/shard_map/bl,btc->ltc/dot_general | solution.py:168
  141.5 1.3 reshape.235
  142.8 2.2 copy.27
  145.0 1.5 reshape.262
  146.5 3.7 %fusion.46 = f32[4,128,512,2,1]{2,1,4,3,0:T(8,128)S(1)} fusion(bf16[512,4,2,128,1]{0,3,2,1,4:T(8,128)(2,1)S(1)} %reshape.262, f32[512,1,512,2]{2,0,3,1:T(8,128)} %get-tuple-element.14, f32[512,1,512,2]{2,0,3,1:T(8,128)} %get-tuple-element.13), kind=kOutput, calls=%fused_computation.85 | convolution fusion | flops 1077936128 | bytes 7340032 | tf_op jit(solution)/shard_map/kpyr,yxrz->kxpz/dot_general | solution.py:97
  150.2 2.3 fusion.32
  152.5 2.5 copy.28
  155.0 1.5 reshape.237.blocks_ref
  156.5 38.1 %shard_map.56 = bf16[128,16,256]{2,1,0:T(8,128)(2,1)} custom-call(bf16[128,16,256]{2,1,0:T(8,128)(2,1)} %reshape.237.blocks_ref), custom_call_target="tpu_custom_call" | custom-call | tf_op jit(solution)/shard_map/pallas_call | solution.py:67
  194.6 1.3 reshape.238
  195.9 1.3 copy.60
  197.3 2.3 reshape.239
  199.5 2.4 copy.45
  202.0 1.0 copy-done.17
  203.0 3.7 %fusion.61 = f32[4,128,512,2,1]{2,1,4,3,0:T(8,128)S(1)} fusion(bf16[4,512,2,128,1]{1,3,2,4,0:T(8,128)(2,1)S(1)} %copy.45, f32[512,1,512,2]{2,0,3,1:T(8,128)} %get-tuple-element.14, f32[512,1,512,2]{2,0,3,1:T(8,128)} %get-tuple-element.13), kind=kOutput, calls=%fused_computation.100 | convolution fusion | flops 1077936128 | bytes 7340032 | tf_op jit(solution)/shard_map/kpxr,yxrz->ykpz/dot_general | solution.py:90
  206.7 2.7 fusion.13
  209.4 0.4 fusion.40
  209.8 1.5 pad_maximum_fusion.6
  211.3 0.2 pad_dynamic-slice_fusion.4
  211.5 2.6 collective-permute-start
  214.1 1.7 pad_dynamic-slice_fusion.5
  215.7 2.0 fusion.24
  217.8 2.8 collective-permute-done
  220.6 3.6 %add_reduce_fusion = f32[4,257,128]{1,2,0:T(8,128)S(1)} fusion(f32[4,257,2,127]{1,3,2,0:T(8,128)} %fusion.24, f32[257]{0:T(512)S(1)} %get-tuple-element.21, s32[]{:T(128)S(6)} %select_n.65, f32[4,512,2,128]{1,3,2,0:T(8,128)S(1)} %copy.19, s32[]{:T(128)S(6)} %add.171, f32[4]{0:T(128)S(1)} %get-tuple-element.22, ...), kind=kLoop, calls=%fused_computation.58 | loop fusion | flops 2763264 | bytes 4989948 | tf_op jit(solution)/shard_map/reduce_sum | solution.py:113
  224.2 0.2 add_sqrt_fusion
  224.4 1.2 copy-done.6
  225.6 3.1 %divide_multiply_fusion.2 = (f32[4,257,2,128]{1,3,2,0:T(8,128)S(1)}, f32[4,257,2,128]{1,3,2,0:T(8,128)}, f32[4,257,2,128]{1,3,2,0:T(8,128)}) fusion(f32[4,257]{1,0:T(4,128)S(1)} %and_convert_fusion, f32[4,257,128]{1,2,0:T(8,128)S(1)} %add_sqrt_fusion, f32[4]{0:T(128)S(1)} %get-tuple-element.22, s32[]{:T(128)S(6)} %select_n.65, ...), kind=kLoop, calls=%fused_computation.57 | loop fusion | flops 2894848 | bytes 8152076 | tf_op jit(solution)/shard_map/mul | solution.py:118
  228.7 1.2 copy-done.8
  230.0 1.9 collective-permute-start.1
  231.9 2.5 slice.90
  234.4 2.7 slice.94
  237.1 47.7 %all-reduce.5.cloned.1.call-done = f32[4,512,2,128]{1,3,2,0:T(8,128)} async-done(((f32[4,512,2,128]{1,3,2,0:T(8,128)}), f32[4,512,2,128]{1,3,2,0:T(8,128)}) %all-reduce.5.cloned.1.call-update) | async-done | bytes 2097168 | tf_op jit(solution)/shard_map/psum | solution.py:189
  284.8 5.4 %fusion.44 = f32[4,256,2,128]{1,3,2,0:T(8,128)} fusion(f32[4,257,2,128]{1,3,2,0:T(8,128)} %get-tuple-element.19, f32[4,257,2,128]{1,3,2,0:T(8,128)} %get-tuple-element.12, f32[4,257,2,128]{1,3,2,0:T(8,128)S(1)} %copy-done.9, f32[3,257,2,128]{1,3,2,0:T(8,128)} %slice.90, f32[1,257,2,128]{1,3,2,0:T(8,128)S(1)} %collective-permute-done.1, ...), kind=kLoop, calls=%fused_computation.78 | loop fusion | flops 2097152 | bytes 8384516 | tf_op jit(solution)/shard_map/add | solution.py:205
  290.2 2.2 copy.33
  (49 shorter events, 0.3 us)
Async XLA Ops:
  6.5 118.4 %copy-start = (bf16[32,128,128]{2,1,0:T(8,128)(2,1)S(1)}, bf16[32,128,128]{2,1,0:T(8,128)(2,1)}, u32[]{:S(2)}) copy-start(bf16[32,128,128]{2,1,0:T(8,128)(2,1)} %param.8) | copy-start | bytes 3145732
  6.5 278.3 %all-reduce.5.cloned.1.call-start = ((), (), s32[]{:S(2)}) async-start(), calls=%async_computation | async-start | bytes 4194304 | tf_op jit(solution)/shard_map/psum | solution.py:189
  35.0 1.8 copy-start.18
  35.0 1.9 copy-start.19
  35.0 2.2 copy-start.20
  35.0 2.5 copy-start.21
  42.0 1.4 copy-start.10
  42.0 2.0 copy-start.12
  106.0 4.0 %copy-start.11 = (f32[512,1,512,2]{2,0,3,1:T(8,128)S(1)}, f32[512,1,512,2]{2,0,3,1:T(8,128)}, u32[]{:S(2)}) copy-start(f32[512,1,512,2]{2,0,3,1:T(8,128)} %copy-done.10) | copy-start | bytes 6291460
  106.0 4.0 %copy-start.13 = (f32[512,1,512,2]{2,0,3,1:T(8,128)S(1)}, f32[512,1,512,2]{2,0,3,1:T(8,128)}, u32[]{:S(2)}) copy-start(f32[512,1,512,2]{2,0,3,1:T(8,128)} %copy-done.12) | copy-start | bytes 6291460
  106.0 4.0 %copy-start.16 = (bf16[512,4,2,128,1]{0,3,2,4,1:T(8,128)(2,1)S(1)}, bf16[512,4,2,128,1]{0,3,2,4,1:T(8,128)(2,1)}, u32[]{:S(2)}) copy-start(bf16[512,4,2,128,1]{0,3,2,4,1:T(8,128)(2,1)} %copy.37) | copy-start | bytes 3145732
  112.3 4.5 %copy-start.22 = (s32[32]{0:T(128)S(1)}, s32[32]{0:T(128)}, u32[]{:S(2)}) copy-start(s32[32]{0:T(128)} %param.9) | copy-start | bytes 388
  146.5 3.7 %copy-start.2 = (f32[512,1,512,2]{2,0,3,1:T(8,128)S(1)}, f32[512,1,512,2]{2,0,3,1:T(8,128)}, u32[]{:S(2)}) copy-start(f32[512,1,512,2]{2,0,3,1:T(8,128)} %get-tuple-element.13) | copy-start | bytes 6291460
  146.5 3.7 %copy-start.4 = (f32[512,1,512,2]{2,0,3,1:T(8,128)S(1)}, f32[512,1,512,2]{2,0,3,1:T(8,128)}, u32[]{:S(2)}) copy-start(f32[512,1,512,2]{2,0,3,1:T(8,128)} %get-tuple-element.14) | copy-start | bytes 6291460
  202.0 1.0 copy-start.17
  203.0 3.7 %copy-start.3 = (f32[512,1,512,2]{2,0,3,1:T(8,128)S(1)}, f32[512,1,512,2]{2,0,3,1:T(8,128)}, u32[]{:S(2)}) copy-start(f32[512,1,512,2]{2,0,3,1:T(8,128)} %get-tuple-element.13) | copy-start | bytes 6291460
  203.0 3.7 %copy-start.5 = (f32[512,1,512,2]{2,0,3,1:T(8,128)S(1)}, f32[512,1,512,2]{2,0,3,1:T(8,128)}, u32[]{:S(2)}) copy-start(f32[512,1,512,2]{2,0,3,1:T(8,128)} %get-tuple-element.14) | copy-start | bytes 6291460
  206.7 2.7 copy-start.14
  206.7 2.7 copy-start.15
  211.5 9.1 %collective-permute-start = (f32[1,258,2,128]{1,3,2,0:T(8,128)S(1)}, f32[1,258,2,128]{1,3,2,0:T(8,128)S(1)}, u32[]{:S(2)}, u32[]{:S(2)}) collective-permute-start(f32[1,258,2,128]{1,3,2,0:T(8,128)S(1)} %pad_dynamic-slice_fusion.4), channel_id=1, source_target_pairs={{2,0},{4,2},{6,4},{8,6},{10,8},{12,10},{14,12},{16,14},{18,16},{20... | collective-permute-start | bytes 792584 | tf_op jit(solution)/shard_map/ppermute | solution.py:21
  220.6 3.8 %copy-start.7 = (f32[4,257,2,127]{1,3,2,0:T(8,128)S(1)}, f32[4,257,2,127]{1,3,2,0:T(8,128)}, u32[]{:S(2)}) copy-start(f32[4,257,2,127]{1,3,2,0:T(8,128)} %fusion.24) | copy-start | bytes 3133348
  224.1 1.4 copy-start.6
  228.7 1.2 copy-start.8
  230.0 7.1 %collective-permute-start.1 = (f32[1,257,2,128]{1,3,2,0:T(8,128)S(1)}, f32[1,257,2,128]{1,3,2,0:T(8,128)S(1)}, u32[]{:S(2)}, u32[]{:S(2)}) collective-permute-start(f32[1,257,2,128]{1,3,2,0:T(8,128)S(1)} %slice.89), channel_id=1, source_target_pairs={{0,2},{2,4},{4,6},{6,8},{8,10},{10,12},{12,14},{14,16},{16,18},{18... | collective-permute-start | bytes 789512 | tf_op jit(solution)/shard_map/ppermute | solution.py:21
  231.9 52.9 %copy-start.9 = (f32[4,257,2,128]{1,3,2,0:T(8,128)S(1)}, f32[4,257,2,128]{1,3,2,0:T(8,128)}, u32[]{:S(2)}) copy-start(f32[4,257,2,128]{1,3,2,0:T(8,128)} %copy-done.8) | copy-start | bytes 3158020
  284.8 7.7 %copy-start.1 = (bf16[32,128,128]{2,1,0:T(8,128)(2,1)S(1)}, bf16[32,128,128]{2,1,0:T(8,128)(2,1)}, u32[]{:S(2)}) copy-start(bf16[32,128,128]{2,1,0:T(8,128)(2,1)} %param.8) | copy-start | bytes 3145732
Sparse Core Ops, SparseCore 0:
  211.4 73.3 all-reduce.4

commit v2 on v0

v2 whole, which is shorter than its diff:
```python
import numpy as np

import jax
import jax.numpy as jnp
from jax import lax
from jax.experimental import pallas as pl
from jax.experimental.pallas import tpu as pltpu
from jax.sharding import PartitionSpec as P

NL = 512
NZ = 128
TILE = 128
PENS = 128
ROWS = 4
BLOCKS = 32
TILES = 16
HALF = NL // 2
PAD = 8
TV_WEIGHT = 2.0
MESH = pl.DeviceIdType.MESH


def dft_table():
    index = np.arange(NL)
    angle = 2.0 * np.pi / NL * (index[:, None] * index[None, :] % NL)
    return np.concatenate([np.cos(angle), np.sin(angle)], 1).astype(jnp.bfloat16)


def split_table():
    table = np.zeros((256, 256), np.float32)
    index = np.arange(128)
    table[index, 2 * index] = 1.0
    table[128 + index, 2 * index + 1] = 1.0
    return table.astype(jnp.bfloat16)


def low_lanes(shape):
    return lax.broadcasted_iota(jnp.int32, shape, len(shape) - 1) < 64


def swap(value):
    return pltpu.roll(value, 64, 1)


def matmul(left, right):
    return jnp.dot(left, right, preferred_element_type=jnp.float32)


def to_messages(result):
    count = result.shape[0] // 8
    groups = [result[:, 128 * a : 128 * (a + 1)].reshape(count, 8, 128) for a in range(4)]
    upper = lax.broadcasted_iota(jnp.int32, (count, 8, 128), 1) < 4
    even, odd = [], []
    for a in (0, 2):
        first, second = groups[a], groups[a + 1]
        even.append(jnp.where(upper, first, pltpu.roll(second, 4, 1)))
        odd.append(jnp.where(upper, pltpu.roll(first, 4, 1), second))
    both = jnp.stack([jnp.concatenate(even, 1), jnp.concatenate(odd, 1)], 1)
    return both.reshape(2 * count, 16, 128).astype(jnp.bfloat16)


def body(
    links,
    image_hbm,
    maps_hbm,
    samples_hbm,
    kernels_hbm,
    table_hbm,
    split_hbm,
    out_ref,
    image,
    maps,
    samples,
    kernels,
    table,
    split,
    planes,
    map_real,
    map_imag,
    packed,
    send_fwd,
    recv_fwd,
    send_back,
    recv_back,
    history,
    gram,
    target,
    wide,
    own_term,
    send_term,
    recv_term,
    tv_part,
    load_sem,
    own_sem,
    fwd_send_sem,
    fwd_recv_sem,
    back_send_sem,
    back_recv_sem,
    term_send_sem,
    term_recv_sem,
    halo_send_sem,
    halo_recv_sem,
):
    me = lax.axis_index("pen")
    coil = lax.axis_index("coil")
    other = 1 - coil
    y, z, rest = me // 64, me // 8 % 8, me % 8

    def partner(i):
        step = i + 1
        dz, more = step % 8, step // 8
        return (y + more // 8) % 2 * 64 + (z + dz) % 8 * 8 + (rest + more % 8) % 8

    pairs = (
        (image_hbm, image),
        (maps_hbm, maps),
        (split_hbm, split),
        (table_hbm, table),
        (kernels_hbm, kernels),
        (samples_hbm, samples),
    )
    loads = [pltpu.make_async_copy(a, b, load_sem.at[i]) for i, (a, b) in enumerate(pairs)]
    for load in loads:
        load.start()

    barrier = pltpu.get_barrier_semaphore()

    def greet(i, carry):
        pl.semaphore_signal(barrier, inc=1, device_id=(partner(i), coil), device_id_type=MESH)
        return carry

    lax.fori_loop(0, PENS - 1, greet, 0)
    pl.semaphore_signal(barrier, inc=1, device_id=(me, other), device_id_type=MESH)

    for load in loads[:3]:
        load.wait()
    planes[:, 1 : ROWS + 1, 0:PAD, :] = jnp.zeros((2, ROWS, PAD, NZ), jnp.float32)
    planes[:, 1 : ROWS + 1, PAD + NL :, :] = jnp.zeros((2, ROWS, PAD, NZ), jnp.float32)

    def coil_block(i, carry):
        row, part = i // 4, i % 4
        start = pl.multiple_of(part * 128, 128)
        low = low_lanes((128, 128))
        pieces = matmul(split[...], maps[row, pl.ds(pl.multiple_of(part * 256, 256), 256), :])
        pieces = pieces * (1.0 / NL)
        real, imag = pieces[:128], pieces[128:]
        real_sw, imag_sw = swap(real), swap(imag)
        field = image.at[row, pl.ds(pl.multiple_of(part * 256, 256), 256), :]
        f_real, f_imag = field[pl.ds(0, 128, 2), :], field[pl.ds(1, 128, 2), :]
        planes[0, row + 1, pl.ds(start + PAD, 128), :] = f_real
        planes[1, row + 1, pl.ds(start + PAD, 128), :] = f_imag
        f_real_sw, f_imag_sw = swap(f_real), swap(f_imag)
        by_half = (
            (jnp.where(low, real, real_sw), jnp.where(low, imag, -imag_sw), jnp.where(low, f_real, f_imag_sw), jnp.where(low, f_imag, f_real_sw)),
            (jnp.where(low, real_sw, real), jnp.where(low, imag_sw, -imag), jnp.where(low, f_real_sw, f_imag), jnp.where(low, f_imag_sw, f_real)),
        )
        for half, (m_real, m_imag, f, f_sw) in enumerate(by_half):
            map_real[half, row, pl.ds(start, 128), :] = m_real.astype(jnp.bfloat16)
            map_imag[half, row, pl.ds(start, 128), :] = m_imag.astype(jnp.bfloat16)
            value = m_real * f - m_imag * f_sw
            turned = swap(value)
            lanes = pl.ds(pl.multiple_of(row * 128, 128), 128)
            packed[half, pl.ds(start, 128), lanes] = value.astype(jnp.bfloat16)
            packed[half, pl.ds(start + NL, 128), lanes] = jnp.where(low, turned, -turned).astype(jnp.bfloat16)
        return carry

    lax.fori_loop(0, 16, coil_block, 0)
    loads[3].wait()

    def to_send(half, send):
        def step(i, carry):
            rows = pl.ds(pl.multiple_of(i * 256, 256), 256)
            send[half, pl.ds(i * 64, 64)] = to_messages(matmul(table[rows, :], packed[half]))
            return carry

        lax.fori_loop(0, 2, step, 0)

    def post(half, send, recv, send_sem, recv_sem, own_index):
        def step(i, carry):
            d = partner(i)
            pltpu.make_async_remote_copy(
                send.at[half, d],
                recv.at[half, me],
                send_sem.at[half],
                recv_sem.at[half],
                device_id=(d, coil),
                device_id_type=MESH,
            ).start()
            return carry

        own = pltpu.make_async_copy(send.at[half, me], recv.at[half, me], own_sem.at[own_index])
        own.start()
        lax.fori_loop(0, PENS - 1, step, 0)
        return own

    def await_all(half, ref, sem):
        part = ref.at[half, pl.ds(0, PENS - 1)]
        pltpu.make_async_copy(part, part, sem.at[half]).wait()

    def unpack(half, recv, sign):
        def widen(i, carry):
            wide[pl.ds(pl.multiple_of(i * 256, 256), 256), :] = (
                recv[half, pl.ds(i * 16, 16)].reshape(256, 128).astype(jnp.float32)
            )
            return carry

        lax.fori_loop(0, 8, widen, 0)
        low = low_lanes((128, 128))
        for a in range(4):
            for part in range(4):
                value = wide[pl.ds(a + 512 * part, 128, 4), :]
                turned = swap(value) * sign
                lanes = slice(a * 128, a * 128 + 128)
                packed[half, 128 * part : 128 * part + 128, lanes] = value.astype(jnp.bfloat16)
                packed[half, NL + 128 * part : NL + 128 * part + 128, lanes] = jnp.where(
                    low, turned, -turned
                ).astype(jnp.bfloat16)

    to_send(0, send_fwd)
    pl.semaphore_wait(barrier, PENS)
    own0 = post(0, send_fwd, recv_fwd, fwd_send_sem, fwd_recv_sem, 0)
    to_send(1, send_fwd)
    own1 = post(1, send_fwd, recv_fwd, fwd_send_sem, fwd_recv_sem, 1)

    window = pl.ds(pl.multiple_of(coil * HALF, HALF), HALF + 2 * PAD)
    halos = []
    for i, (source, place, to) in enumerate(((1, ROWS + 1, me + PENS - 1), (ROWS, 0, me + 1))):
        halo = pltpu.make_async_remote_copy(
            planes.at[:, source, window],
            planes.at[:, place, window],
            halo_send_sem.at[i],
            halo_recv_sem.at[i],
            device_id=(to % PENS, coil),
            device_id_type=MESH,
        )
        halo.start()
        halos.append(halo)

    loads[4].wait()
    loads[5].wait()
    history[0] = jnp.zeros((TILE, 3 * 128), jnp.float32)

    def chain(i, carry):
        weights = kernels[i]
        pieces = matmul(split[...], samples[i]).astype(jnp.bfloat16)
        right = jnp.concatenate([weights, pieces[:128], pieces[128:]], 1)
        term = lax.dot_general(weights, right, (((0,), (0,)), ((), ())), preferred_element_type=jnp.float32)
        history[i + 1] = history[links[i]] + term
        return carry

    lax.fori_loop(0, BLOCKS, chain, 0)

    def finish(tile, carry):
        total = history[links[BLOCKS + tile]]
        low = low_lanes((128, 128))
        gram[tile] = total[:, :128].astype(jnp.bfloat16)
        real, imag = total[:, 128:256], total[:, 256:]
        target[0, tile] = jnp.where(low, real, swap(imag))
        target[1, tile] = jnp.where(low, swap(real), imag)
        return carry

    lax.fori_loop(0, TILES, finish, 0)

    def grid_side(half, own):
        await_all(half, recv_fwd, fwd_recv_sem)
        own.wait()
        unpack(half, recv_fwd, 1.0)
        low = low_lanes((128, 128))
        spectrum = []
        for i in range(2):
            spectrum.append(matmul(table[256 * i : 256 * i + 256, :], packed[half]).astype(jnp.bfloat16))
        for i in range(2):
            for k in range(2):
                quarter = 2 * i + k
                for column in range(4):
                    lanes = slice(column * 128, column * 128 + 128)
                    cells = spectrum[i][128 * k : 128 * k + 128, lanes]
                    tile = 4 * column + quarter
                    value = matmul(gram[tile], cells) - target[half, tile]
                    turned = swap(value)
                    packed[half, 128 * quarter : 128 * quarter + 128, lanes] = value.astype(jnp.bfloat16)
                    packed[half, NL + 128 * quarter : NL + 128 * quarter + 128, lanes] = jnp.where(
                        low, -turned, turned
                    ).astype(jnp.bfloat16)
        to_send(half, send_back)
        return post(half, send_back, recv_back, back_send_sem, back_recv_sem, 2 + half)

    own2 = grid_side(0, own0)

    for halo in halos:
        halo.wait_recv()
    first_col = coil * HALF

    def tv_columns(i, carry):
        lane = lax.broadcasted_iota(jnp.int32, (72, 128), 1)
        cols = lax.broadcasted_iota(jnp.int32, (72, 128), 0) + (first_col + i * 64 - PAD)
        col_ok = jnp.logical_and(cols >= 0, cols != NL - 1)
        start = pl.multiple_of(first_col + i * 64, 64)

        def tv_row(k, before):
            row = me * ROWS + k - 1
            row_ok = jnp.logical_and(row >= 0, row != NL - 1).astype(jnp.float32)
            diffs, squares = [], 1.0
            for r in range(2):
                here = planes[r, k, pl.ds(start, 80), :]
                above = planes[r, k + 1, pl.ds(start, 72), :]
                center = here[:72]
                diff_y = (above - center) * row_ok
                diff_x = jnp.where(col_ok, here[1:73] - center, 0.0)
                diff_z = jnp.where(lane == NZ - 1, 0.0, pltpu.roll(center, NZ - 1, 1) - center)
                squares = squares + (diff_y * diff_y + diff_x * diff_x + diff_z * diff_z)
                diffs.append((diff_y, diff_x, diff_z))
            inverse = TV_WEIGHT / jnp.sqrt(squares)
            after = []
            for r in range(2):
                flux_y, flux_x, flux_z = (diff * inverse for diff in diffs[r])
                flux_y, flux_z = flux_y[8:], flux_z[8:]
                shifted = jnp.where(lane[8:] == 0, 0.0, pltpu.roll(flux_z, 1, 1))
                tv_part[k, r, pl.ds(pl.multiple_of(i * 64, 64), 64), :] = (
                    before[r] - flux_y + flux_x[7:71] - flux_x[8:] + shifted - flux_z
                )
                after.append(flux_y)
            return tuple(after)

        zero = jnp.zeros((64, 128), jnp.float32)
        lax.fori_loop(0, ROWS + 1, tv_row, (zero, zero))
        return carry

    lax.fori_loop(0, HALF // 64, tv_columns, 0)

    own3 = grid_side(1, own1)

    def coil_terms(half, side):
        columns = pl.ds(pl.multiple_of(side * HALF, HALF), HALF)
        result = matmul(table[columns, :], packed[half])
        for row in range(ROWS):
            value = result[:, row * 128 : row * 128 + 128]
            real = map_real[half, row, columns, :].astype(jnp.float32)
            imag = map_imag[half, row, columns, :].astype(jnp.float32)
            yield row, real * value + imag * swap(value)

    def image_side(half, own):
        await_all(half, recv_back, back_recv_sem)
        own.wait()
        unpack(half, recv_back, -1.0)
        for row, term in coil_terms(half, other):
            send_term[half, row] = term.astype(jnp.bfloat16)
        copy = pltpu.make_async_remote_copy(
            send_term.at[half],
            recv_term.at[half],
            term_send_sem.at[half],
            term_recv_sem.at[half],
            device_id=(me, other),
            device_id_type=MESH,
        )
        copy.start()
        for row, term in coil_terms(half, coil):
            own_term[half, row] = term
        return copy

    copies = [image_side(0, own2), image_side(1, own3)]
    for halo in halos:
        halo.wait_send()
    for half in range(2):
        await_all(half, send_fwd, fwd_send_sem)
        await_all(half, send_back, back_send_sem)
    for copy in copies:
        copy.wait()

    def combine(row, carry):
        low = low_lanes((HALF, 128))
        first = own_term[0, row] + recv_term[0, row].astype(jnp.float32)
        second = own_term[1, row] + recv_term[1, row].astype(jnp.float32)
        out_ref[row, pl.ds(0, HALF, 2), :] = jnp.where(low, first, swap(second)) + tv_part[row + 1, 0]
        out_ref[row, pl.ds(1, HALF, 2), :] = jnp.where(low, swap(first), second) + tv_part[row + 1, 1]
        return carry

    lax.fori_loop(0, ROWS, combine, 0)


def on_device(image_field, coil_maps, samples, kernels, tile_of_block):
    ids = tile_of_block % TILES
    place = jnp.arange(BLOCKS, dtype=jnp.int32)
    wanted = jnp.concatenate([ids, jnp.arange(TILES, dtype=jnp.int32)])
    limit = jnp.minimum(jnp.arange(BLOCKS + TILES, dtype=jnp.int32), BLOCKS)
    hits = jnp.logical_and(wanted[:, None] == ids[None, :], place[None, :] < limit[:, None])
    links = jnp.max(jnp.where(hits, place[None, :] + 1, 0), axis=1)
    bf16, f32 = jnp.bfloat16, jnp.float32
    dma = pltpu.SemaphoreType.DMA
    hbm = pl.BlockSpec(memory_space=pl.ANY)
    out = pl.pallas_call(
        body,
        out_shape=jax.ShapeDtypeStruct((ROWS, 2 * HALF, NZ), f32),
        in_specs=[pl.BlockSpec(memory_space=pltpu.SMEM)] + [hbm] * 6,
        out_specs=pl.BlockSpec(memory_space=pltpu.VMEM),
        scratch_shapes=[
            pltpu.VMEM((ROWS, 2 * NL, NZ), f32),
            pltpu.VMEM((ROWS, 2 * NL, NZ), bf16),
            pltpu.VMEM((BLOCKS, 256, NZ), bf16),
            pltpu.VMEM((BLOCKS, TILE, TILE), bf16),
            pltpu.VMEM((NL, 2 * NL), bf16),
            pltpu.VMEM((256, 256), bf16),
            pltpu.VMEM((2, ROWS + 2, NL + 2 * PAD, NZ), f32),
            pltpu.VMEM((2, ROWS, NL, NZ), bf16),
            pltpu.VMEM((2, ROWS, NL, NZ), bf16),
            pltpu.VMEM((2, 2 * NL, 4 * 128), bf16),
            pltpu.VMEM((2, PENS, 16, 128), bf16),
            pltpu.VMEM((2, PENS, 16, 128), bf16),
            pltpu.VMEM((2, PENS, 16, 128), bf16),
            pltpu.VMEM((2, PENS, 16, 128), bf16),
            pltpu.VMEM((BLOCKS + 1, TILE, 3 * 128), f32),
            pltpu.VMEM((TILES, TILE, TILE), bf16),
            pltpu.VMEM((2, TILES, TILE, 128), f32),
            pltpu.VMEM((PENS * 16, 128), f32),
            pltpu.VMEM((2, ROWS, HALF, 128), f32),
            pltpu.VMEM((2, ROWS, HALF, 128), bf16),
            pltpu.VMEM((2, ROWS, HALF, 128), bf16),
            pltpu.VMEM((ROWS + 1, 2, HALF, 128), f32),
            dma((6,)),
            dma((4,)),
            dma((2,)),
            dma((2,)),
            dma((2,)),
            dma((2,)),
            dma((2,)),
            dma((2,)),
            dma((2,)),
            dma((2,)),
        ],
        compiler_params=pltpu.CompilerParams(
            collective_id=0, has_side_effects=True, vmem_limit_bytes=56 << 20
        ),
        name="adjoint_gradient",
    )(
        links,
        image_field.reshape(ROWS, 2 * NL, NZ),
        coil_maps.reshape(ROWS, 2 * NL, NZ),
        samples.reshape(BLOCKS, 256, NZ),
        kernels,
        jnp.asarray(dft_table()),
        jnp.asarray(split_table()),
    )
    return out.reshape(ROWS, HALF, 2, NZ)


def solution(mesh):
    in_specs = (
        P("pen", None, None, None),
        P("coil", "pen", None, None, None),
        P("coil", "pen", None, None, None),
        P("pen", None, None),
        P("pen"),
    )
    out_specs = P("pen", "coil", None, None)
    return jax.shard_map(
        on_device, mesh=mesh, in_specs=in_specs, out_specs=out_specs, check_vma=False
    )
```

time: 272 us -> 83.9 us (0.31)
  waiting for transfers between devices: 103 us -> 0 us
  Pallas kernels: 0 us -> 80.1 us
  local copies, waits for them, and re-layouts: 64.8 us -> 2.27 us
  other arithmetic: 36.7 us -> 1.35 us
  matrix products: 26.8 us -> 0 us
  starting transfers between devices: 26.6 us -> 0 us
  between operations: 13.7 us -> 0.01 us
    pallas_call x0 -> x1, Pallas kernels: none -> 80.1 us  [on_device(): pl.pallas_call(body, out_shape=jax.ShapeDtypeStruct((ROWS, 2 * HALF, NZ),...]
    all_to_all x2 -> x0, waiting for transfers between devices: 55.4 us -> none  [the longest x1 29.4 us: on_device(): lax.all_to_all(back_rows, 'pen', split_axis=0, concat_axis=1, tiled=True)]
    psum x1 -> x0, waiting for transfers between devices: 47.2 us -> none  [on_device(): summed = lax.psum(coil_term, 'coil')]
    dot_general x10 -> x0, matrix products: 26.8 us -> none  [the longest x1 6.36 us: on_device(): jnp.einsum('bst,bsc->btc', kernels, misfit, preferred_element_type=jnp.fl...]
    all_to_all x2 -> x0, starting transfers between devices: 22.4 us -> none  [the longest x1 16.9 us: on_device(): lax.all_to_all(rows_spectrum, 'pen', split_axis=1, concat_axis=0, tiled=T...]
    convert_element_type x3 -> x0, local copies, waits for them, and re-layouts: 14 us -> none  [the longest x1 6.67 us: on_device(): measured = samples[0].reshape(predicted.shape).astype(jnp.float32)]
    unnamed x45 -> x1, local copies, waits for them, and re-layouts: 15.1 us -> 2.26 us
    slice x5 -> x0, local copies, waits for them, and re-layouts: 10.4 us -> none  [the longest x1 4.27 us: on_device(): map_real = coil_maps[0, :, :, 0].astype(jnp.float32)]
  transfers between devices with their start and end apart: 5 -> 0, of which waited for: 3 -> 0; matrix products, arithmetic and copies ran while one was open for 11% -> 0% of each run, Pallas kernels for 0% -> 0%
where the time goes in v2:
time: 83.9 us; the launch traced here: 83.8 us
  Pallas kernels  80.1 us (95%)
  local copies, waits for them, and re-layouts  2.27 us (3%)
  other arithmetic  1.35 us (2%)
    pallas_call x1, Pallas kernels, on_device(): pl.pallas_call(body, out_shape=jax.ShapeDtypeStruct((ROWS, 2 * HALF, NZ),...  80.1 us
    unnamed x1, local copies, waits for them, and re-layouts  2.26 us

profile of v2, /device:TPU:1, one launch (start us, length us, event | category | flops | bytes accessed | tf_op | source)
XLA Modules:
  0.0 83.8 jit_solution(6056144430263008584)
XLA Ops:
  0.0 0.7 and_select_fusion
  0.7 0.1 pad_add_fusion
  0.7 0.6 select_reduce_fusion.links
  1.4 80.1 %adjoint_gradient.1 = f32[4,512,128]{2,1,0:T(8,128)} custom-call(s32[48]{0:T(128)} %select_reduce_fusion.links, f32[4,1024,128]{2,1,0:T(8,128)} %bitcast.5, bf16[4,1024,128]{2,1,0:T(8,128)(2,1)} %bitcast.7, bf16[32,256,128]{2,1,0:T(8,128)(2,1)} %bitcast.6, bf16[32,128,128]{2,1,0:T(8,128)(2,1)} %kernels_hbm.1, bf16[512,1024]{1,0:T(8,128)(2,1)} %constant.26.clone.table_hbm, ...), custom_call_target="tpu_custom_call" | custom-call | tf_op jit(solution)/shard_map/adjoint_gradient/pallas_call | solution.py:391
  81.5 2.3 %copy.9 = f32[4,256,2,128]{3,2,1,0:T(2,128)} copy(f32[4,256,2,128]{3,2,1,0:T(2,128)} %bitcast.4) | data formatting | bytes 2097152
  (2 shorter events, 0.0 us)

commit v3 on v2

--- a/solution.py
+++ b/solution.py
@@ -60,14 +60,15 @@
 
 
 def body(
-    links,
+    tile_ids,
     image_hbm,
     maps_hbm,
     samples_hbm,
     kernels_hbm,
     table_hbm,
     split_hbm,
-    out_ref,
+    data_out,
+    tv_out,
     image,
     maps,
     samples,
@@ -90,6 +91,9 @@
     send_term,
     recv_term,
     tv_part,
+    data_part,
+    links_vector,
+    links,
     load_sem,
     own_sem,
     fwd_send_sem,
@@ -98,18 +102,27 @@
     back_recv_sem,
     term_send_sem,
     term_recv_sem,
+    store_sem,
     halo_send_sem,
     halo_recv_sem,
+    links_sem,
 ):
     me = lax.axis_index("pen")
     coil = lax.axis_index("coil")
     other = 1 - coil
     y, z, rest = me // 64, me // 8 % 8, me % 8
-
-    def partner(i):
-        step = i + 1
-        dz, more = step % 8, step // 8
-        return (y + more // 8) % 2 * 64 + (z + dz) % 8 * 8 + (rest + more % 8) % 8
+    ring = [(z + d) % 8 * 8 for d in (4, 3, 5, 2, 6, 1, 7, 0)]
+
+    def for_partners(act):
+        def group(i, carry):
+            base = (y + 1 - i // 8) % 2 * 64 + (rest + 15 - i) % 8
+            for place in ring:
+                act(base + place)
+            return carry
+
+        lax.fori_loop(0, 15, group, 0)
+        for place in ring[:7]:
+            act(y * 64 + rest + place)
 
     pairs = (
         (image_hbm, image),
@@ -125,12 +138,24 @@
 
     barrier = pltpu.get_barrier_semaphore()
 
-    def greet(i, carry):
-        pl.semaphore_signal(barrier, inc=1, device_id=(partner(i), coil), device_id_type=MESH)
-        return carry
-
-    lax.fori_loop(0, PENS - 1, greet, 0)
+    def greet(d):
+        pl.semaphore_signal(barrier, inc=1, device_id=(d, coil), device_id_type=MESH)
+
+    for_partners(greet)
     pl.semaphore_signal(barrier, inc=1, device_id=(me, other), device_id_type=MESH)
+
+    ids = jnp.broadcast_to(tile_ids[...] % TILES, (BLOCKS, BLOCKS))
+    place = lax.broadcasted_iota(jnp.int32, (BLOCKS, BLOCKS), 1)
+    line = lax.broadcasted_iota(jnp.int32, (BLOCKS, BLOCKS), 0)
+    own_id = jnp.max(jnp.where(place == line, ids, 0), axis=1, keepdims=True)
+    before = jnp.where(jnp.logical_and(ids == own_id, place < line), place + 1, 0)
+    last = jnp.where(ids == line, place + 1, 0)
+    for i, found in enumerate((before, last)):
+        links_vector[BLOCKS * i : BLOCKS * i + BLOCKS, :] = jnp.broadcast_to(
+            jnp.max(found, axis=1, keepdims=True), (BLOCKS, 128)
+        )
+    links_copy = pltpu.make_async_copy(links_vector, links, links_sem)
+    links_copy.start()
 
     for load in loads[:3]:
         load.wait()
@@ -176,8 +201,7 @@
         lax.fori_loop(0, 2, step, 0)
 
     def post(half, send, recv, send_sem, recv_sem, own_index):
-        def step(i, carry):
-            d = partner(i)
+        def step(d):
             pltpu.make_async_remote_copy(
                 send.at[half, d],
                 recv.at[half, me],
@@ -186,11 +210,10 @@
                 device_id=(d, coil),
                 device_id_type=MESH,
             ).start()
-            return carry
 
         own = pltpu.make_async_copy(send.at[half, me], recv.at[half, me], own_sem.at[own_index])
         own.start()
-        lax.fori_loop(0, PENS - 1, step, 0)
+        for_partners(step)
         return own
 
     def await_all(half, ref, sem):
@@ -238,6 +261,7 @@
 
     loads[4].wait()
     loads[5].wait()
+    links_copy.wait()
     history[0] = jnp.zeros((TILE, 3 * 128), jnp.float32)
 
     def chain(i, carry):
@@ -245,13 +269,13 @@
         pieces = matmul(split[...], samples[i]).astype(jnp.bfloat16)
         right = jnp.concatenate([weights, pieces[:128], pieces[128:]], 1)
         term = lax.dot_general(weights, right, (((0,), (0,)), ((), ())), preferred_element_type=jnp.float32)
-        history[i + 1] = history[links[i]] + term
+        history[i + 1] = history[jnp.clip(links[i, 0], 0, BLOCKS)] + term
         return carry
 
     lax.fori_loop(0, BLOCKS, chain, 0)
 
     def finish(tile, carry):
-        total = history[links[BLOCKS + tile]]
+        total = history[jnp.clip(links[BLOCKS + tile, 0], 0, BLOCKS)]
         low = low_lanes((128, 128))
         gram[tile] = total[:, :128].astype(jnp.bfloat16)
         real, imag = total[:, 128:256], total[:, 256:]
@@ -316,7 +340,7 @@
                 flux_y, flux_x, flux_z = (diff * inverse for diff in diffs[r])
                 flux_y, flux_z = flux_y[8:], flux_z[8:]
                 shifted = jnp.where(lane[8:] == 0, 0.0, pltpu.roll(flux_z, 1, 1))
-                tv_part[k, r, pl.ds(pl.multiple_of(i * 64, 64), 64), :] = (
+                tv_part[k, pl.ds(pl.multiple_of(i * 128, 128) + r, 64, 2), :] = (
                     before[r] - flux_y + flux_x[7:71] - flux_x[8:] + shifted - flux_z
                 )
                 after.append(flux_y)
@@ -327,6 +351,8 @@
         return carry
 
     lax.fori_loop(0, HALF // 64, tv_columns, 0)
+    tv_store = pltpu.make_async_copy(tv_part.at[pl.ds(1, ROWS)], tv_out, store_sem.at[ROWS])
+    tv_store.start()
 
     own3 = grid_side(1, own1)
 
@@ -343,56 +369,57 @@
         await_all(half, recv_back, back_recv_sem)
         own.wait()
         unpack(half, recv_back, -1.0)
+        copies = []
         for row, term in coil_terms(half, other):
             send_term[half, row] = term.astype(jnp.bfloat16)
-        copy = pltpu.make_async_remote_copy(
-            send_term.at[half],
-            recv_term.at[half],
-            term_send_sem.at[half],
-            term_recv_sem.at[half],
-            device_id=(me, other),
-            device_id_type=MESH,
-        )
-        copy.start()
+            copy = pltpu.make_async_remote_copy(
+                send_term.at[half, row],
+                recv_term.at[half, row],
+                term_send_sem.at[half, row],
+                term_recv_sem.at[half, row],
+                device_id=(me, other),
+                device_id_type=MESH,
+            )
+            copy.start()
+            copies.append(copy)
         for row, term in coil_terms(half, coil):
             own_term[half, row] = term
-        return copy
-
-    copies = [image_side(0, own2), image_side(1, own3)]
+        return copies
+
+    first_copies = image_side(0, own2)
+    second_copies = image_side(1, own3)
     for halo in halos:
         halo.wait_send()
     for half in range(2):
         await_all(half, send_fwd, fwd_send_sem)
         await_all(half, send_back, back_send_sem)
-    for copy in copies:
-        copy.wait()
-
-    def combine(row, carry):
-        low = low_lanes((HALF, 128))
+    tv_store.wait()
+
+    stores = []
+    low = low_lanes((HALF, 128))
+    for row in range(ROWS):
+        first_copies[row].wait()
+        second_copies[row].wait()
         first = own_term[0, row] + recv_term[0, row].astype(jnp.float32)
         second = own_term[1, row] + recv_term[1, row].astype(jnp.float32)
-        out_ref[row, pl.ds(0, HALF, 2), :] = jnp.where(low, first, swap(second)) + tv_part[row + 1, 0]
-        out_ref[row, pl.ds(1, HALF, 2), :] = jnp.where(low, swap(first), second) + tv_part[row + 1, 1]
-        return carry
-
-    lax.fori_loop(0, ROWS, combine, 0)
+        data_part[row, pl.ds(0, HALF, 2), :] = jnp.where(low, first, swap(second))
+        data_part[row, pl.ds(1, HALF, 2), :] = jnp.where(low, swap(first), second)
+        store = pltpu.make_async_copy(data_part.at[row], data_out.at[row], store_sem.at[row])
+        store.start()
+        stores.append(store)
+    for store in stores:
+        store.wait()
 
 
 def on_device(image_field, coil_maps, samples, kernels, tile_of_block):
-    ids = tile_of_block % TILES
-    place = jnp.arange(BLOCKS, dtype=jnp.int32)
-    wanted = jnp.concatenate([ids, jnp.arange(TILES, dtype=jnp.int32)])
-    limit = jnp.minimum(jnp.arange(BLOCKS + TILES, dtype=jnp.int32), BLOCKS)
-    hits = jnp.logical_and(wanted[:, None] == ids[None, :], place[None, :] < limit[:, None])
-    links = jnp.max(jnp.where(hits, place[None, :] + 1, 0), axis=1)
     bf16, f32 = jnp.bfloat16, jnp.float32
     dma = pltpu.SemaphoreType.DMA
     hbm = pl.BlockSpec(memory_space=pl.ANY)
-    out = pl.pallas_call(
+    data_part, tv_part = pl.pallas_call(
         body,
-        out_shape=jax.ShapeDtypeStruct((ROWS, 2 * HALF, NZ), f32),
-        in_specs=[pl.BlockSpec(memory_space=pltpu.SMEM)] + [hbm] * 6,
-        out_specs=pl.BlockSpec(memory_space=pltpu.VMEM),
+        out_shape=[jax.ShapeDtypeStruct((ROWS, 2 * HALF, NZ), f32)] * 2,
+        in_specs=[pl.BlockSpec(memory_space=pltpu.VMEM)] + [hbm] * 6,
+        out_specs=[hbm] * 2,
         scratch_shapes=[
             pltpu.VMEM((ROWS, 2 * NL, NZ), f32),
             pltpu.VMEM((ROWS, 2 * NL, NZ), bf16),
@@ -415,24 +442,29 @@
             pltpu.VMEM((2, ROWS, HALF, 128), f32),
             pltpu.VMEM((2, ROWS, HALF, 128), bf16),
             pltpu.VMEM((2, ROWS, HALF, 128), bf16),
-            pltpu.VMEM((ROWS + 1, 2, HALF, 128), f32),
+            pltpu.VMEM((ROWS + 1, 2 * HALF, 128), f32),
+            pltpu.VMEM((ROWS, 2 * HALF, 128), f32),
+            pltpu.VMEM((2 * BLOCKS, 128), jnp.int32),
+            pltpu.SMEM((2 * BLOCKS, 128), jnp.int32),
             dma((6,)),
             dma((4,)),
             dma((2,)),
             dma((2,)),
             dma((2,)),
             dma((2,)),
-            dma((2,)),
-            dma((2,)),
-            dma((2,)),
-            dma((2,)),
+            dma((2, ROWS)),
+            dma((2, ROWS)),
+            dma((ROWS + 1,)),
+            dma((2,)),
+            dma((2,)),
+            dma(()),
         ],
         compiler_params=pltpu.CompilerParams(
             collective_id=0, has_side_effects=True, vmem_limit_bytes=56 << 20
         ),
         name="adjoint_gradient",
     )(
-        links,
+        tile_of_block.reshape(1, BLOCKS),
         image_field.reshape(ROWS, 2 * NL, NZ),
         coil_maps.reshape(ROWS, 2 * NL, NZ),
         samples.reshape(BLOCKS, 256, NZ),
@@ -440,7 +472,7 @@
         jnp.asarray(dft_table()),
         jnp.asarray(split_table()),
     )
-    return out.reshape(ROWS, HALF, 2, NZ)
+    return (data_part + tv_part).reshape(ROWS, HALF, 2, NZ)
 
 
 def solution(mesh):

time: 83.9 us -> 78.6 us (0.937)
  Pallas kernels: 80.1 us -> 75.8 us
  local copies, waits for them, and re-layouts: 2.27 us -> 0 us
  other arithmetic: 1.35 us -> 2.62 us
    pallas_call x1, Pallas kernels: 80.1 us -> 75.8 us  [on_device(): pl.pallas_call(body, out_shape=[jax.ShapeDtypeStruct((ROWS, 2 * HALF, NZ)...]
    add x0 -> x1, other arithmetic: none -> 2.62 us  [on_device(): return (data_part + tv_part).reshape(ROWS, HALF, 2, NZ)]
    unnamed x1 -> x0, local copies, waits for them, and re-layouts: 2.26 us -> none
where the time goes in v3:
time: 78.6 us; the launch traced here: 78.5 us
  Pallas kernels  75.8 us (96%)
  other arithmetic  2.62 us (3%)
    pallas_call x1, Pallas kernels, on_device(): pl.pallas_call(body, out_shape=[jax.ShapeDtypeStruct((ROWS, 2 * HALF, NZ)...  75.8 us
    add x1, other arithmetic, on_device(): return (data_part + tv_part).reshape(ROWS, HALF, 2, NZ)  2.62 us

profile of v3, /device:TPU:1, one launch (start us, length us, event | category | flops | bytes accessed | tf_op | source)
XLA Modules:
  0.0 78.5 jit_solution(8600937743593387500)
XLA Ops:
  0.0 75.8 %adjoint_gradient.1 = (f32[4,512,128]{2,1,0:T(8,128)}, f32[4,512,128]{2,1,0:T(8,128)}) custom-call(s32[1,32]{1,0:T(1,128)} %bitcast.8, f32[4,1024,128]{2,1,0:T(8,128)} %bitcast.5, bf16[4,1024,128]{2,1,0:T(8,128)(2,1)} %bitcast.7, bf16[32,256,128]{2,1,0:T(8,128)(2,1)} %bitcast.6, bf16[32,128,128]{2,1,0:T(8,128)(2,1)} %kernels_hbm.1, ...), custom_call_target="tpu_custom_call" | custom-call | tf_op jit(solution)/shard_map/adjoint_gradient/pallas_call | solution.py:418
  75.8 2.6 %add.3 = f32[4,512,128]{2,1,0:T(8,128)} add(f32[4,512,128]{2,1,0:T(8,128)} %get-tuple-element.7, f32[4,512,128]{2,1,0:T(8,128)} %get-tuple-element.8) | non-fusion elementwise | flops 262144 | bytes 3145728 | tf_op jit(solution)/shard_map/add | solution.py:475

commit v4 on v3

--- a/solution.py
+++ b/solution.py
@@ -92,6 +92,8 @@
     recv_term,
     tv_part,
     data_part,
+    halo_out,
+    halo_in,
     links_vector,
     links,
     load_sem,
@@ -247,10 +249,11 @@
 
     window = pl.ds(pl.multiple_of(coil * HALF, HALF), HALF + 2 * PAD)
     halos = []
-    for i, (source, place, to) in enumerate(((1, ROWS + 1, me + PENS - 1), (ROWS, 0, me + 1))):
+    for i, (source, to) in enumerate(((1, me + PENS - 1), (ROWS, me + 1))):
+        halo_out[i] = planes[:, source, window, :].astype(jnp.bfloat16)
         halo = pltpu.make_async_remote_copy(
-            planes.at[:, source, window],
-            planes.at[:, place, window],
+            halo_out.at[i],
+            halo_in.at[i],
             halo_send_sem.at[i],
             halo_recv_sem.at[i],
             device_id=(to % PENS, coil),
@@ -311,8 +314,11 @@
 
     own2 = grid_side(0, own0)
 
-    for halo in halos:
-        halo.wait_recv()
+    own3 = grid_side(1, own1)
+
+    for i, place in enumerate((ROWS + 1, 0)):
+        halos[i].wait_recv()
+        planes[:, place, window, :] = halo_in[i].astype(jnp.float32)
     first_col = coil * HALF
 
     def tv_columns(i, carry):
@@ -353,8 +359,6 @@
     lax.fori_loop(0, HALF // 64, tv_columns, 0)
     tv_store = pltpu.make_async_copy(tv_part.at[pl.ds(1, ROWS)], tv_out, store_sem.at[ROWS])
     tv_store.start()
-
-    own3 = grid_side(1, own1)
 
     def coil_terms(half, side):
         columns = pl.ds(pl.multiple_of(side * HALF, HALF), HALF)
@@ -444,6 +448,8 @@
             pltpu.VMEM((2, ROWS, HALF, 128), bf16),
             pltpu.VMEM((ROWS + 1, 2 * HALF, 128), f32),
             pltpu.VMEM((ROWS, 2 * HALF, 128), f32),
+            pltpu.VMEM((2, 2, HALF + 2 * PAD, 128), bf16),
+            pltpu.VMEM((2, 2, HALF + 2 * PAD, 128), bf16),
             pltpu.VMEM((2 * BLOCKS, 128), jnp.int32),
             pltpu.SMEM((2 * BLOCKS, 128), jnp.int32),
             dma((6,)),

time: 78.6 us -> 77 us (0.980)
  Pallas kernels: 75.8 us -> 73.9 us
    pallas_call x1, Pallas kernels: 75.8 us -> 73.9 us  [on_device(): pl.pallas_call(body, out_shape=[jax.ShapeDtypeStruct((ROWS, 2 * HALF, NZ)...]
where the time goes in v4:
time: 77 us; the launch traced here: 76.5 us
  Pallas kernels  73.9 us (96%)
  other arithmetic  2.62 us (3%)
    pallas_call x1, Pallas kernels, on_device(): pl.pallas_call(body, out_shape=[jax.ShapeDtypeStruct((ROWS, 2 * HALF, NZ)...  73.9 us
    add x1, other arithmetic, on_device(): return (data_part + tv_part).reshape(ROWS, HALF, 2, NZ)  2.62 us

profile of v4, /device:TPU:1, one launch (start us, length us, event | category | flops | bytes accessed | tf_op | source)
XLA Modules:
  0.0 76.5 jit_solution(7544129236542476860)
XLA Ops:
  0.0 73.9 %adjoint_gradient.1 = (f32[4,512,128]{2,1,0:T(8,128)}, f32[4,512,128]{2,1,0:T(8,128)}) custom-call(s32[1,32]{1,0:T(1,128)} %bitcast.8, f32[4,1024,128]{2,1,0:T(8,128)} %bitcast.5, bf16[4,1024,128]{2,1,0:T(8,128)(2,1)} %bitcast.7, bf16[32,256,128]{2,1,0:T(8,128)(2,1)} %bitcast.6, bf16[32,128,128]{2,1,0:T(8,128)(2,1)} %kernels_hbm.1, ...), custom_call_target="tpu_custom_call" | custom-call | tf_op jit(solution)/shard_map/adjoint_gradient/pallas_call | solution.py:422
  73.9 2.6 %add.3 = f32[4,512,128]{2,1,0:T(8,128)} add(f32[4,512,128]{2,1,0:T(8,128)} %get-tuple-element.7, f32[4,512,128]{2,1,0:T(8,128)} %get-tuple-element.8) | non-fusion elementwise | flops 262144 | bytes 3145728 | tf_op jit(solution)/shard_map/add | solution.py:481

commit v5 on v4

--- a/solution.py
+++ b/solution.py
@@ -222,16 +222,17 @@
         part = ref.at[half, pl.ds(0, PENS - 1)]
         pltpu.make_async_copy(part, part, sem.at[half]).wait()
 
-    def unpack(half, recv, sign):
+    def unpack(half, recv, sign, groups=range(4), load=True):
         def widen(i, carry):
             wide[pl.ds(pl.multiple_of(i * 256, 256), 256), :] = (
                 recv[half, pl.ds(i * 16, 16)].reshape(256, 128).astype(jnp.float32)
             )
             return carry
 
-        lax.fori_loop(0, 8, widen, 0)
+        if load:
+            lax.fori_loop(0, 8, widen, 0)
         low = low_lanes((128, 128))
-        for a in range(4):
+        for a in groups:
             for part in range(4):
                 value = wide[pl.ds(a + 512 * part, 128, 4), :]
                 turned = swap(value) * sign
@@ -360,11 +361,12 @@
     tv_store = pltpu.make_async_copy(tv_part.at[pl.ds(1, ROWS)], tv_out, store_sem.at[ROWS])
     tv_store.start()
 
-    def coil_terms(half, side):
+    def coil_terms(half, side, pair):
         columns = pl.ds(pl.multiple_of(side * HALF, HALF), HALF)
-        result = matmul(table[columns, :], packed[half])
-        for row in range(ROWS):
-            value = result[:, row * 128 : row * 128 + 128]
+        result = matmul(table[columns, :], packed[half, :, 256 * pair : 256 * pair + 256])
+        for i in range(2):
+            row = 2 * pair + i
+            value = result[:, i * 128 : i * 128 + 128]
             real = map_real[half, row, columns, :].astype(jnp.float32)
             imag = map_imag[half, row, columns, :].astype(jnp.float32)
             yield row, real * value + imag * swap(value)
@@ -372,22 +374,24 @@
     def image_side(half, own):
         await_all(half, recv_back, back_recv_sem)
         own.wait()
-        unpack(half, recv_back, -1.0)
         copies = []
-        for row, term in coil_terms(half, other):
-            send_term[half, row] = term.astype(jnp.bfloat16)
-            copy = pltpu.make_async_remote_copy(
-                send_term.at[half, row],
-                recv_term.at[half, row],
-                term_send_sem.at[half, row],
-                term_recv_sem.at[half, row],
-                device_id=(me, other),
-                device_id_type=MESH,
-            )
-            copy.start()
-            copies.append(copy)
-        for row, term in coil_terms(half, coil):
-            own_term[half, row] = term
+        for pair in range(2):
+            unpack(half, recv_back, -1.0, (2 * pair, 2 * pair + 1), pair == 0)
+            for row, term in coil_terms(half, other, pair):
+                send_term[half, row] = term.astype(jnp.bfloat16)
+                copy = pltpu.make_async_remote_copy(
+                    send_term.at[half, row],
+                    recv_term.at[half, row],
+                    term_send_sem.at[half, row],
+                    term_recv_sem.at[half, row],
+                    device_id=(me, other),
+                    device_id_type=MESH,
+                )
+                copy.start()
+                copies.append(copy)
+        for pair in range(2):
+            for row, term in coil_terms(half, coil, pair):
+                own_term[half, row] = term
         return copies
 
     first_copies = image_side(0, own2)

time: 77 us -> 76.7 us (level)
  no operation moved by 1% of the time
where the time goes in v5:
time: 76.7 us; the launch traced here: 76.2 us
  Pallas kernels  73.6 us (96%)
  other arithmetic  2.62 us (3%)
    pallas_call x1, Pallas kernels, on_device(): pl.pallas_call(body, out_shape=[jax.ShapeDtypeStruct((ROWS, 2 * HALF, NZ)...  73.6 us
    add x1, other arithmetic, on_device(): return (data_part + tv_part).reshape(ROWS, HALF, 2, NZ)  2.62 us

profile of v5, /device:TPU:1, one launch (start us, length us, event | category | flops | bytes accessed | tf_op | source)
XLA Modules:
  0.0 76.2 jit_solution(566721078889287542)
XLA Ops:
  0.0 73.6 %adjoint_gradient.1 = (f32[4,512,128]{2,1,0:T(8,128)}, f32[4,512,128]{2,1,0:T(8,128)}) custom-call(s32[1,32]{1,0:T(1,128)} %bitcast.8, f32[4,1024,128]{2,1,0:T(8,128)} %bitcast.5, bf16[4,1024,128]{2,1,0:T(8,128)(2,1)} %bitcast.7, bf16[32,256,128]{2,1,0:T(8,128)(2,1)} %bitcast.6, bf16[32,128,128]{2,1,0:T(8,128)(2,1)} %kernels_hbm.1, ...), custom_call_target="tpu_custom_call" | custom-call | tf_op jit(solution)/shard_map/adjoint_gradient/pallas_call | solution.py:426
  73.6 2.6 %add.3 = f32[4,512,128]{2,1,0:T(8,128)} add(f32[4,512,128]{2,1,0:T(8,128)} %get-tuple-element.7, f32[4,512,128]{2,1,0:T(8,128)} %get-tuple-element.8) | non-fusion elementwise | flops 262144 | bytes 3145728 | tf_op jit(solution)/shard_map/add | solution.py:485
